TPU v7x, 32 devices: a whole 2x2x4 slice. The times are simulated.
32 devices in a mesh: depth: 2 (over x), strip: 16 (over z, y, core).
Axes of the slice: x: 2, y: 2, z: 4, core: 2. Of those that a mesh axis runs over, the one named last changes fastest.
Arguments:
- surface: float32 [2, 4, 256, 1024], P(None, None, 'strip'), may hold values from -6 to 6
- velocity_class: int32 [2, 256, 1024], P('depth', 'strip'), may hold values from 0 to 7
- table: float32 [2, 8, 2, 10], replicated, may hold values from -2 to 2
Outputs:
- image: float32 [2, 256, 1024], P('depth', 'strip')
All inputs are finite; a program needn't handle non-finite values.
Results may differ from a plain program's by a relative error of at most 0.00017.
Values sent between devices are 32-bit elements; how exact they have to be, the bound alone decides.
A program may use at most 64 MiB of HBM per device.

v0:
```python
import jax
import jax.numpy as jnp
from jax import lax
from jax.sharding import PartitionSpec as P

PASSES = 9
CLASSES = 8


def extended(shard, sides, width):
    for axis, dim in sides:
        devices, length = (lax.axis_size(axis), shard.shape[dim])
        up = [(i, (i + 1) % devices) for i in range(devices - 1)]
        down = [(j, i) for i, j in up]
        last = lax.slice_in_dim(shard, length - width, length, axis=dim)
        initial = lax.slice_in_dim(shard, 0, width, axis=dim)
        before = lax.ppermute(last, axis, up)
        after = lax.ppermute(initial, axis, down)
        shard = jnp.concatenate([before, shard, after], axis=dim)
    return shard


def mcclellan(field):
    lead = [(0, 0)] * (field.ndim - 2)
    padded = jnp.pad(field, lead + [(1, 1), (1, 1)])
    beside = (
        padded[..., 2:, 1:-1]
        + padded[..., :-2, 1:-1]
        + padded[..., 1:-1, 2:]
        + padded[..., 1:-1, :-2]
    )
    corners = (
        padded[..., 2:, 2:] + padded[..., 2:, :-2] + padded[..., :-2, 2:] + padded[..., :-2, :-2]
    )
    return -0.5 * field + 0.25 * beside + 0.125 * corners


def weigh(result, field, real_part, imag_part):
    return jnp.stack(
        [
            result[:, 0] + (real_part * field[:, 0] - imag_part * field[:, 1]),
            result[:, 1] + (real_part * field[:, 1] + imag_part * field[:, 0]),
            result[:, 2] + (real_part * field[:, 2] + imag_part * field[:, 3]),
            result[:, 3] + (real_part * field[:, 3] - imag_part * field[:, 2]),
        ],
        axis=1,
    )


def correlate(fields):
    total = jnp.zeros(fields.shape[2:], jnp.float32)
    for freq_index in range(fields.shape[0]):
        total = total + (
            fields[freq_index, 0] * fields[freq_index, 2]
            + fields[freq_index, 1] * fields[freq_index, 3]
        )
    return total


def tile_halo(sending, rim_width):
    return extended(sending, (("depth", 4), ("strip", 3)), rim_width)


def clip_domain(field, rim_width):
    row_count = field.shape[-2] - 2 * rim_width
    row_ids = (
        lax.axis_index("strip") * row_count
        - rim_width
        + jnp.arange(field.shape[-2], dtype=jnp.int32)
    )
    keep = ((row_ids >= 0) & (row_ids < row_count * lax.axis_size("strip")))[:, None]
    col_count = field.shape[-1] - 2 * rim_width
    col_ids = (
        lax.axis_index("depth") * col_count
        - rim_width
        + jnp.arange(field.shape[-1], dtype=jnp.int32)
    )
    keep = keep & ((col_ids >= 0) & (col_ids < col_count * lax.axis_size("depth")))[None, :]
    return jnp.where(keep, field, 0.0)


def chebyshev(fields, onehot, table_part, rim_width, widen):
    row_count = fields.shape[-2]
    col_count = fields.shape[-1]

    def coefficients(degree):
        pair = jnp.einsum(
            "cij,fcp->fpij", onehot, table_part[:, :, :, degree], precision=lax.Precision.HIGHEST
        )
        return (pair[:, 0], pair[:, 1])

    real_part, imag_part = coefficients(0)
    result = weigh(jnp.zeros_like(fields), fields, real_part, imag_part)
    sending = fields[None]
    widened = widen(sending, rim_width)
    wide_prev = widened[0]
    wide_curr = widened[-1]
    for inner_pass in range(rim_width):
        degree = inner_pass
        if degree == 0:
            following = mcclellan(wide_curr)
        else:
            following = 2.0 * mcclellan(wide_curr) - wide_prev
        following = clip_domain(following, rim_width)
        wide_prev, wide_curr = (wide_curr, following)
        real_part, imag_part = coefficients(degree + 1)
        inner = wide_curr[..., rim_width : rim_width + row_count, :]
        inner = inner[..., rim_width : rim_width + col_count]
        result = weigh(result, inner, real_part, imag_part)
    return result


def body(surface, velocity_class, table):
    classes = jnp.arange(CLASSES, dtype=jnp.int32)
    rim_width = PASSES
    velocity = lax.all_to_all(velocity_class, "depth", split_axis=2, concat_axis=0, tiled=True)
    col_count = velocity.shape[2]
    fields = lax.dynamic_slice_in_dim(surface, lax.axis_index("depth") * col_count, col_count, 3)

    def descend(level_index, state_pair):
        level_fields, image = state_pair
        classes_here = lax.dynamic_index_in_dim(velocity, level_index, 0, keepdims=False)
        onehot = (classes_here[None] == classes[:, None, None]).astype(jnp.float32)
        level_fields = chebyshev(level_fields, onehot, table, rim_width, tile_halo)
        image = lax.dynamic_update_index_in_dim(image, correlate(level_fields), level_index, 0)
        return (level_fields, image)

    initial = (fields, jnp.zeros((velocity.shape[0], velocity.shape[1], col_count), jnp.float32))
    fields, image = lax.fori_loop(0, velocity.shape[0], descend, initial)
    return lax.all_to_all(image, "depth", split_axis=0, concat_axis=2, tiled=True)


def solution(mesh):
    in_specs = (P(None, None, "strip", None), P("depth", "strip", None), P())
    out_specs = P("depth", "strip", None)
    return jax.shard_map(body, mesh=mesh, in_specs=in_specs, out_specs=out_specs, check_vma=False)
```

profile of v0, /device:TPU:16, one launch (start us, length us, event | category | flops | bytes accessed | tf_op | source)
XLA Modules:
  0.0 130.6 jit_solution(17852371826067644041)
XLA Ops:
  4.6 3.3 %all-to-all-start = ((s32[2,1,8192]{2,1,0:T(1,128)}), s32[2,1,8192]{2,1,0:T(1,128)S(1)}, u32[]{:S(2)}, u32[]{:S(2)}) async-start(s32[2,1,8192]{2,1,0:T(1,128)} %reshape.214), calls=%async_computation | async-start | bytes 131072 | tf_op jit(solution)/shard_map/all_to_all | solution.py:116
  8.7 3.2 %all-to-all-done = s32[2,1,8192]{2,1,0:T(1,128)S(1)} async-done(((s32[2,1,8192]{2,1,0:T(1,128)}), s32[2,1,8192]{2,1,0:T(1,128)S(1)}, u32[]{:S(2)}, u32[]{:S(2)}) %all-to-all-start) | async-done | bytes 65568 | tf_op jit(solution)/shard_map/all_to_all | solution.py:116
  14.0 109.5 %while.19 = (s32[]{:T(128)}, f32[2,4,16,512]{3,1,0,2:T(4,128)S(1)}, f32[2,16,512]{2,1,0:T(8,128)S(1)}, s32[2,16,512]{2,0,1:T(2,128)S(1)}, f32[2,8,2,10]{1,2,0,3:...) while((s32[]{:T(128)}, f32[2,4,16,512]{3,1,0,2:T(4,128)S(1)}, ...), condition=%wide.region_1.2_spmd.clone, body=%wide.region_0.1_spmd.clone.sunk | while | flops 55837504 | bytes 32179936 | solution.py:129
  15.6 4.5 %collective-permute-start.1 = (f32[1,2,4,16,9]{4,2,1,3,0:T(4,128)S(1)}, f32[1,2,4,16,9]{4,2,1,3,0:T(4,128)S(1)}, u32[]{:S(2)}, u32[]{:S(2)}) collective-permute-start(f32[1,2,4,16,9]{4,2,1,3,0:T(4,128)S(1)} %get-tuple-element.263), channel_id=1, source_target_pairs={{0,16},{1,17},{2,18},{3,19},{4,20},{5,21},{6,22},{7,23},{8,24},{9,... | collective-permute-start | bytes 13832 | tf_op jit(solution)/shard_map/while/body/eval_jaxpr/ppermute | solution.py:17
  26.1 2.4 %collective-permute-start.3 = (f32[1,2,4,9,530]{4,2,1,3,0:T(4,128)S(1)}, f32[1,2,4,9,530]{4,2,1,3,0:T(4,128)S(1)}, u32[]{:S(2)}, u32[]{:S(2)}) collective-permute-start(f32[1,2,4,9,530]{4,2,1,3,0:T(4,128)S(1)} %get-tuple-element.265), channel_id=1, source_target_pairs={{0,1},{1,2},{2,3},{3,4},{4,5},{5,6},{6,7},{7,8},{8,9},{9,10},{10,1... | collective-permute-start | bytes 457928 | tf_op jit(solution)/shard_map/while/body/eval_jaxpr/ppermute | solution.py:17
  29.1 4.7 %collective-permute-done.3 = f32[1,2,4,9,530]{4,2,1,3,0:T(4,128)S(1)} collective-permute-done((f32[1,2,4,9,530]{4,2,1,3,0:T(4,128)S(1)}, f32[1,2,4,9,530]{4,2,1,3,0:T(4,128)S(1)}, u32[]{:S(2)}, u32[]{:S(2)}) %collective-permute-start.3) | collective-permute-done | bytes 152672 | tf_op jit(solution)/shard_map/while/body/eval_jaxpr/ppermute | solution.py:17
  36.3 2.8 %subtract_select_fusion.16 = f32[2,4,34,530]{3,1,0,2:T(4,128)S(1)} fusion(f32[2,4,34,530]{3,1,0,2:T(4,128)S(1)} %add_select_fusion.2, pred[34,530]{1,0:T(8,128)(4,1)S(1)} %broadcast_and_fusion.2, f32[1,2,4,9,530]{4,2,1,3,0:T(4,128)S(1)} %collective-permute-done.2, f32[1,2,4,16,9]{4,2,1,3,0:T(4,128)S(1)} %collective-permute-done, ...), kind=kLoop, calls=%fused_computation.19.clone.1 | loop fusion | flops 2594880 | bytes 1747940 | tf_op jit(solution)/shard_map/while/body/eval_jaxpr/jit(_where)/select_n | solution.py:79
  39.1 4.6 %subtract_select_fusion.17 = f32[2,4,34,530]{3,1,0,2:T(4,128)S(1)} fusion(f32[2,4,34,530]{3,1,0,2:T(4,128)S(1)} %subtract_select_fusion.16, pred[34,530]{1,0:T(8,128)(4,1)S(1)} %broadcast_and_fusion.2, f32[2,4,34,530]{3,1,0,2:T(4,128)S(1)} %maximum_bitcast_fusion.2), kind=kLoop, calls=%fused_computation.18.clone.1 | loop fusion | flops 3748160 | bytes 1747940 | tf_op jit(solution)/shard_map/while/body/eval_jaxpr/jit(_where)/select_n | solution.py:79
  43.8 2.2 %subtract_select_fusion.18 = f32[2,4,34,530]{3,1,0,2:T(4,128)S(1)} fusion(f32[2,4,34,530]{3,1,0,2:T(4,128)S(1)} %subtract_select_fusion.16, f32[2,4,34,530]{3,1,0,2:T(4,128)S(1)} %subtract_select_fusion.17, pred[34,530]{1,0:T(8,128)(4,1)S(1)} %broadcast_and_fusion.2), kind=kLoop, calls=%fused_computation.17.clone.1 | loop fusion | flops 2018240 | bytes 1747940 | tf_op jit(solution)/shard_map/while/body/eval_jaxpr/jit(_where)/select_n | solution.py:79
  46.0 2.2 %subtract_select_fusion.19 = f32[2,4,34,530]{3,1,0,2:T(4,128)S(1)} fusion(f32[2,4,34,530]{3,1,0,2:T(4,128)S(1)} %subtract_select_fusion.17, f32[2,4,34,530]{3,1,0,2:T(4,128)S(1)} %subtract_select_fusion.18, pred[34,530]{1,0:T(8,128)(4,1)S(1)} %broadcast_and_fusion.2), kind=kLoop, calls=%fused_computation.16.clone.1 | loop fusion | flops 2018240 | bytes 1747940 | tf_op jit(solution)/shard_map/while/body/eval_jaxpr/jit(_where)/select_n | solution.py:79
  48.1 2.2 %subtract_select_fusion.20 = f32[2,4,34,530]{3,1,0,2:T(4,128)S(1)} fusion(f32[2,4,34,530]{3,1,0,2:T(4,128)S(1)} %subtract_select_fusion.18, f32[2,4,34,530]{3,1,0,2:T(4,128)S(1)} %subtract_select_fusion.19, pred[34,530]{1,0:T(8,128)(4,1)S(1)} %broadcast_and_fusion.2), kind=kLoop, calls=%fused_computation.15.clone.1 | loop fusion | flops 2018240 | bytes 1747940 | tf_op jit(solution)/shard_map/while/body/eval_jaxpr/jit(_where)/select_n | solution.py:79
  50.3 2.2 %subtract_select_fusion.21 = f32[2,4,34,530]{3,1,0,2:T(4,128)S(1)} fusion(f32[2,4,34,530]{3,1,0,2:T(4,128)S(1)} %subtract_select_fusion.19, f32[2,4,34,530]{3,1,0,2:T(4,128)S(1)} %subtract_select_fusion.20, pred[34,530]{1,0:T(8,128)(4,1)S(1)} %broadcast_and_fusion.2), kind=kLoop, calls=%fused_computation.14.clone.1 | loop fusion | flops 2018240 | bytes 1747940 | tf_op jit(solution)/shard_map/while/body/eval_jaxpr/jit(_where)/select_n | solution.py:79
  52.5 2.2 %subtract_select_fusion.22 = f32[2,4,34,530]{3,1,0,2:T(4,128)S(1)} fusion(f32[2,4,34,530]{3,1,0,2:T(4,128)S(1)} %subtract_select_fusion.20, f32[2,4,34,530]{3,1,0,2:T(4,128)S(1)} %subtract_select_fusion.21, pred[34,530]{1,0:T(8,128)(4,1)S(1)} %broadcast_and_fusion.2), kind=kLoop, calls=%fused_computation.13.clone.1 | loop fusion | flops 2018240 | bytes 1747940 | tf_op jit(solution)/shard_map/while/body/eval_jaxpr/jit(_where)/select_n | solution.py:79
  56.9 2.7 %subtract_add_fusion.5 = f32[2,1,16,512]{3,1,0,2:T(1,128)S(1)} fusion(f32[2,4,34,530]{3,1,0,2:T(4,128)S(1)} %subtract_select_fusion.23, f32[2,4,34,530]{3,1,0,2:T(4,128)S(1)} %subtract_select_fusion.22, f32[2,4,34,530]{3,1,0,2:T(4,128)S(1)} %subtract_select_fusion.21, f32[2,4,34,530]{3,1,0,2:T(4,128)S(1)} %subtract_select_fusion.20, ...), kind=kLoop, calls=%fused_computation.38.clone.1 | loop fusion | flops 638976 | bytes 2686976 | tf_op jit(solution)/shard_map/while/body/eval_jaxpr/add | solution.py:41
  59.6 2.7 %add_add_fusion.5 = f32[2,1,16,512]{3,1,0,2:T(1,128)S(1)} fusion(f32[2,4,34,530]{3,1,0,2:T(4,128)S(1)} %subtract_select_fusion.23, f32[2,4,34,530]{3,1,0,2:T(4,128)S(1)} %subtract_select_fusion.22, f32[2,4,34,530]{3,1,0,2:T(4,128)S(1)} %subtract_select_fusion.21, f32[2,4,34,530]{3,1,0,2:T(4,128)S(1)} %subtract_select_fusion.20, ...), kind=kLoop, calls=%fused_computation.37.clone.1 | loop fusion | flops 638976 | bytes 2686976 | tf_op jit(solution)/shard_map/while/body/eval_jaxpr/add | solution.py:42
  62.3 3.1 %add_add_fusion.4 = f32[2,1,16,512]{3,1,0,2:T(1,128)S(1)} fusion(f32[2,4,34,530]{3,1,0,2:T(4,128)S(1)} %subtract_select_fusion.23, f32[2,4,34,530]{3,1,0,2:T(4,128)S(1)} %subtract_select_fusion.22, f32[2,4,34,530]{3,1,0,2:T(4,128)S(1)} %subtract_select_fusion.21, f32[2,4,34,530]{3,1,0,2:T(4,128)S(1)} %subtract_select_fusion.20, ...), kind=kLoop, calls=%fused_computation.36.clone.1 | loop fusion | flops 638976 | bytes 2686976 | tf_op jit(solution)/shard_map/while/body/eval_jaxpr/add | solution.py:43
  65.4 3.0 %subtract_add_fusion.4 = f32[2,1,16,512]{3,1,0,2:T(1,128)S(1)} fusion(f32[2,4,34,530]{3,1,0,2:T(4,128)S(1)} %subtract_select_fusion.23, f32[2,4,34,530]{3,1,0,2:T(4,128)S(1)} %subtract_select_fusion.22, f32[2,4,34,530]{3,1,0,2:T(4,128)S(1)} %subtract_select_fusion.21, f32[2,4,34,530]{3,1,0,2:T(4,128)S(1)} %subtract_select_fusion.20, ...), kind=kLoop, calls=%fused_computation.35.clone.1 | loop fusion | flops 638976 | bytes 2686976 | tf_op jit(solution)/shard_map/while/body/eval_jaxpr/add | solution.py:44
  70.2 4.5 %collective-permute-start.1 = (f32[1,2,4,16,9]{4,2,1,3,0:T(4,128)S(1)}, f32[1,2,4,16,9]{4,2,1,3,0:T(4,128)S(1)}, u32[]{:S(2)}, u32[]{:S(2)}) collective-permute-start(f32[1,2,4,16,9]{4,2,1,3,0:T(4,128)S(1)} %get-tuple-element.263), channel_id=1, source_target_pairs={{0,16},{1,17},{2,18},{3,19},{4,20},{5,21},{6,22},{7,23},{8,24},{9,... | collective-permute-start | bytes 13832 | tf_op jit(solution)/shard_map/while/body/eval_jaxpr/ppermute | solution.py:17
  80.8 2.4 %collective-permute-start.3 = (f32[1,2,4,9,530]{4,2,1,3,0:T(4,128)S(1)}, f32[1,2,4,9,530]{4,2,1,3,0:T(4,128)S(1)}, u32[]{:S(2)}, u32[]{:S(2)}) collective-permute-start(f32[1,2,4,9,530]{4,2,1,3,0:T(4,128)S(1)} %get-tuple-element.265), channel_id=1, source_target_pairs={{0,1},{1,2},{2,3},{3,4},{4,5},{5,6},{6,7},{7,8},{8,9},{9,10},{10,1... | collective-permute-start | bytes 457928 | tf_op jit(solution)/shard_map/while/body/eval_jaxpr/ppermute | solution.py:17
  83.8 4.7 %collective-permute-done.3 = f32[1,2,4,9,530]{4,2,1,3,0:T(4,128)S(1)} collective-permute-done((f32[1,2,4,9,530]{4,2,1,3,0:T(4,128)S(1)}, f32[1,2,4,9,530]{4,2,1,3,0:T(4,128)S(1)}, u32[]{:S(2)}, u32[]{:S(2)}) %collective-permute-start.3) | collective-permute-done | bytes 152672 | tf_op jit(solution)/shard_map/while/body/eval_jaxpr/ppermute | solution.py:17
  91.0 2.8 %subtract_select_fusion.16 = f32[2,4,34,530]{3,1,0,2:T(4,128)S(1)} fusion(f32[2,4,34,530]{3,1,0,2:T(4,128)S(1)} %add_select_fusion.2, pred[34,530]{1,0:T(8,128)(4,1)S(1)} %broadcast_and_fusion.2, f32[1,2,4,9,530]{4,2,1,3,0:T(4,128)S(1)} %collective-permute-done.2, f32[1,2,4,16,9]{4,2,1,3,0:T(4,128)S(1)} %collective-permute-done, ...), kind=kLoop, calls=%fused_computation.19.clone.1 | loop fusion | flops 2594880 | bytes 1747940 | tf_op jit(solution)/shard_map/while/body/eval_jaxpr/jit(_where)/select_n | solution.py:79
  93.8 4.6 %subtract_select_fusion.17 = f32[2,4,34,530]{3,1,0,2:T(4,128)S(1)} fusion(f32[2,4,34,530]{3,1,0,2:T(4,128)S(1)} %subtract_select_fusion.16, pred[34,530]{1,0:T(8,128)(4,1)S(1)} %broadcast_and_fusion.2, f32[2,4,34,530]{3,1,0,2:T(4,128)S(1)} %maximum_bitcast_fusion.2), kind=kLoop, calls=%fused_computation.18.clone.1 | loop fusion | flops 3748160 | bytes 1747940 | tf_op jit(solution)/shard_map/while/body/eval_jaxpr/jit(_where)/select_n | solution.py:79
  98.4 2.2 %subtract_select_fusion.18 = f32[2,4,34,530]{3,1,0,2:T(4,128)S(1)} fusion(f32[2,4,34,530]{3,1,0,2:T(4,128)S(1)} %subtract_select_fusion.16, f32[2,4,34,530]{3,1,0,2:T(4,128)S(1)} %subtract_select_fusion.17, pred[34,530]{1,0:T(8,128)(4,1)S(1)} %broadcast_and_fusion.2), kind=kLoop, calls=%fused_computation.17.clone.1 | loop fusion | flops 2018240 | bytes 1747940 | tf_op jit(solution)/shard_map/while/body/eval_jaxpr/jit(_where)/select_n | solution.py:79
  100.6 2.2 %subtract_select_fusion.19 = f32[2,4,34,530]{3,1,0,2:T(4,128)S(1)} fusion(f32[2,4,34,530]{3,1,0,2:T(4,128)S(1)} %subtract_select_fusion.17, f32[2,4,34,530]{3,1,0,2:T(4,128)S(1)} %subtract_select_fusion.18, pred[34,530]{1,0:T(8,128)(4,1)S(1)} %broadcast_and_fusion.2), kind=kLoop, calls=%fused_computation.16.clone.1 | loop fusion | flops 2018240 | bytes 1747940 | tf_op jit(solution)/shard_map/while/body/eval_jaxpr/jit(_where)/select_n | solution.py:79
  102.8 2.2 %subtract_select_fusion.20 = f32[2,4,34,530]{3,1,0,2:T(4,128)S(1)} fusion(f32[2,4,34,530]{3,1,0,2:T(4,128)S(1)} %subtract_select_fusion.18, f32[2,4,34,530]{3,1,0,2:T(4,128)S(1)} %subtract_select_fusion.19, pred[34,530]{1,0:T(8,128)(4,1)S(1)} %broadcast_and_fusion.2), kind=kLoop, calls=%fused_computation.15.clone.1 | loop fusion | flops 2018240 | bytes 1747940 | tf_op jit(solution)/shard_map/while/body/eval_jaxpr/jit(_where)/select_n | solution.py:79
  105.0 2.2 %subtract_select_fusion.21 = f32[2,4,34,530]{3,1,0,2:T(4,128)S(1)} fusion(f32[2,4,34,530]{3,1,0,2:T(4,128)S(1)} %subtract_select_fusion.19, f32[2,4,34,530]{3,1,0,2:T(4,128)S(1)} %subtract_select_fusion.20, pred[34,530]{1,0:T(8,128)(4,1)S(1)} %broadcast_and_fusion.2), kind=kLoop, calls=%fused_computation.14.clone.1 | loop fusion | flops 2018240 | bytes 1747940 | tf_op jit(solution)/shard_map/while/body/eval_jaxpr/jit(_where)/select_n | solution.py:79
  107.2 2.2 %subtract_select_fusion.22 = f32[2,4,34,530]{3,1,0,2:T(4,128)S(1)} fusion(f32[2,4,34,530]{3,1,0,2:T(4,128)S(1)} %subtract_select_fusion.20, f32[2,4,34,530]{3,1,0,2:T(4,128)S(1)} %subtract_select_fusion.21, pred[34,530]{1,0:T(8,128)(4,1)S(1)} %broadcast_and_fusion.2), kind=kLoop, calls=%fused_computation.13.clone.1 | loop fusion | flops 2018240 | bytes 1747940 | tf_op jit(solution)/shard_map/while/body/eval_jaxpr/jit(_where)/select_n | solution.py:79
  111.6 2.7 %subtract_add_fusion.5 = f32[2,1,16,512]{3,1,0,2:T(1,128)S(1)} fusion(f32[2,4,34,530]{3,1,0,2:T(4,128)S(1)} %subtract_select_fusion.23, f32[2,4,34,530]{3,1,0,2:T(4,128)S(1)} %subtract_select_fusion.22, f32[2,4,34,530]{3,1,0,2:T(4,128)S(1)} %subtract_select_fusion.21, f32[2,4,34,530]{3,1,0,2:T(4,128)S(1)} %subtract_select_fusion.20, ...), kind=kLoop, calls=%fused_computation.38.clone.1 | loop fusion | flops 638976 | bytes 2686976 | tf_op jit(solution)/shard_map/while/body/eval_jaxpr/add | solution.py:41
  114.3 2.7 %add_add_fusion.5 = f32[2,1,16,512]{3,1,0,2:T(1,128)S(1)} fusion(f32[2,4,34,530]{3,1,0,2:T(4,128)S(1)} %subtract_select_fusion.23, f32[2,4,34,530]{3,1,0,2:T(4,128)S(1)} %subtract_select_fusion.22, f32[2,4,34,530]{3,1,0,2:T(4,128)S(1)} %subtract_select_fusion.21, f32[2,4,34,530]{3,1,0,2:T(4,128)S(1)} %subtract_select_fusion.20, ...), kind=kLoop, calls=%fused_computation.37.clone.1 | loop fusion | flops 638976 | bytes 2686976 | tf_op jit(solution)/shard_map/while/body/eval_jaxpr/add | solution.py:42
  117.0 3.1 %add_add_fusion.4 = f32[2,1,16,512]{3,1,0,2:T(1,128)S(1)} fusion(f32[2,4,34,530]{3,1,0,2:T(4,128)S(1)} %subtract_select_fusion.23, f32[2,4,34,530]{3,1,0,2:T(4,128)S(1)} %subtract_select_fusion.22, f32[2,4,34,530]{3,1,0,2:T(4,128)S(1)} %subtract_select_fusion.21, f32[2,4,34,530]{3,1,0,2:T(4,128)S(1)} %subtract_select_fusion.20, ...), kind=kLoop, calls=%fused_computation.36.clone.1 | loop fusion | flops 638976 | bytes 2686976 | tf_op jit(solution)/shard_map/while/body/eval_jaxpr/add | solution.py:43
  120.0 3.0 %subtract_add_fusion.4 = f32[2,1,16,512]{3,1,0,2:T(1,128)S(1)} fusion(f32[2,4,34,530]{3,1,0,2:T(4,128)S(1)} %subtract_select_fusion.23, f32[2,4,34,530]{3,1,0,2:T(4,128)S(1)} %subtract_select_fusion.22, f32[2,4,34,530]{3,1,0,2:T(4,128)S(1)} %subtract_select_fusion.21, f32[2,4,34,530]{3,1,0,2:T(4,128)S(1)} %subtract_select_fusion.20, ...), kind=kLoop, calls=%fused_computation.35.clone.1 | loop fusion | flops 638976 | bytes 2686976 | tf_op jit(solution)/shard_map/while/body/eval_jaxpr/add | solution.py:44
  123.5 6.5 %all_to_all.36 = f32[2,16,512]{2,1,0:T(8,128)S(1)} all-to-all(f32[2,16,512]{2,1,0:T(8,128)S(1)} %get-tuple-element.180), channel_id=1, replica_groups=mesh['depth'=2,'strip'=16] {'depth'}, dimensions={0} | all-to-all | bytes 131072 | tf_op jit(solution)/shard_map/all_to_all | solution.py:130
  (74 shorter events, 33.6 us)
Async XLA Ops:
  0.0 7.9 %copy-start = (f32[2,4,16,1024]{3,2,1,0:T(8,128)S(1)}, f32[2,4,16,1024]{3,2,1,0:T(8,128)}, u32[]{:S(2)}) copy-start(f32[2,4,16,1024]{3,2,1,0:T(8,128)} %param.5) | copy-start | bytes 1572868
  4.6 7.4 %all-to-all-start = ((s32[2,1,8192]{2,1,0:T(1,128)}), s32[2,1,8192]{2,1,0:T(1,128)S(1)}, u32[]{:S(2)}, u32[]{:S(2)}) async-start(s32[2,1,8192]{2,1,0:T(1,128)} %reshape.214), calls=%async_computation | async-start | bytes 131072 | tf_op jit(solution)/shard_map/all_to_all | solution.py:116
  7.9 0.7 copy-start.1
  14.3 9.5 %collective-permute-start = (f32[1,2,4,16,9]{4,2,1,3,0:T(4,128)S(1)}, f32[1,2,4,16,9]{4,2,1,3,0:T(4,128)S(1)}, u32[]{:S(2)}, u32[]{:S(2)}) collective-permute-start(f32[1,2,4,16,9]{4,2,1,3,0:T(4,128)S(1)} %get-tuple-element.262), channel_id=1, source_target_pairs={{16,0},{17,1},{18,2},{19,3},{20,4},{21,5},{22,6},{23,7},{24,8},{25... | collective-permute-start | bytes 13832 | tf_op jit(solution)/shard_map/while/body/eval_jaxpr/ppermute | solution.py:18
  15.6 8.3 %collective-permute-start.1 = (f32[1,2,4,16,9]{4,2,1,3,0:T(4,128)S(1)}, f32[1,2,4,16,9]{4,2,1,3,0:T(4,128)S(1)}, u32[]{:S(2)}, u32[]{:S(2)}) collective-permute-start(f32[1,2,4,16,9]{4,2,1,3,0:T(4,128)S(1)} %get-tuple-element.263), channel_id=1, source_target_pairs={{0,16},{1,17},{2,18},{3,19},{4,20},{5,21},{6,22},{7,23},{8,24},{9,... | collective-permute-start | bytes 13832 | tf_op jit(solution)/shard_map/while/body/eval_jaxpr/ppermute | solution.py:17
  24.2 5.0 %collective-permute-start.2 = (f32[1,2,4,9,530]{4,2,1,3,0:T(4,128)S(1)}, f32[1,2,4,9,530]{4,2,1,3,0:T(4,128)S(1)}, u32[]{:S(2)}, u32[]{:S(2)}) collective-permute-start(f32[1,2,4,9,530]{4,2,1,3,0:T(4,128)S(1)} %get-tuple-element.264), channel_id=1, source_target_pairs={{1,0},{2,1},{3,2},{4,3},{5,4},{6,5},{7,6},{8,7},{9,8},{10,9},{11,1... | collective-permute-start | bytes 457928 | tf_op jit(solution)/shard_map/while/body/eval_jaxpr/ppermute | solution.py:18
  26.1 7.8 %collective-permute-start.3 = (f32[1,2,4,9,530]{4,2,1,3,0:T(4,128)S(1)}, f32[1,2,4,9,530]{4,2,1,3,0:T(4,128)S(1)}, u32[]{:S(2)}, u32[]{:S(2)}) collective-permute-start(f32[1,2,4,9,530]{4,2,1,3,0:T(4,128)S(1)} %get-tuple-element.265), channel_id=1, source_target_pairs={{0,1},{1,2},{2,3},{3,4},{4,5},{5,6},{6,7},{7,8},{8,9},{9,10},{10,1... | collective-permute-start | bytes 457928 | tf_op jit(solution)/shard_map/while/body/eval_jaxpr/ppermute | solution.py:17
  68.9 9.5 %collective-permute-start = (f32[1,2,4,16,9]{4,2,1,3,0:T(4,128)S(1)}, f32[1,2,4,16,9]{4,2,1,3,0:T(4,128)S(1)}, u32[]{:S(2)}, u32[]{:S(2)}) collective-permute-start(f32[1,2,4,16,9]{4,2,1,3,0:T(4,128)S(1)} %get-tuple-element.262), channel_id=1, source_target_pairs={{16,0},{17,1},{18,2},{19,3},{20,4},{21,5},{22,6},{23,7},{24,8},{25... | collective-permute-start | bytes 13832 | tf_op jit(solution)/shard_map/while/body/eval_jaxpr/ppermute | solution.py:18
  70.2 8.3 %collective-permute-start.1 = (f32[1,2,4,16,9]{4,2,1,3,0:T(4,128)S(1)}, f32[1,2,4,16,9]{4,2,1,3,0:T(4,128)S(1)}, u32[]{:S(2)}, u32[]{:S(2)}) collective-permute-start(f32[1,2,4,16,9]{4,2,1,3,0:T(4,128)S(1)} %get-tuple-element.263), channel_id=1, source_target_pairs={{0,16},{1,17},{2,18},{3,19},{4,20},{5,21},{6,22},{7,23},{8,24},{9,... | collective-permute-start | bytes 13832 | tf_op jit(solution)/shard_map/while/body/eval_jaxpr/ppermute | solution.py:17
  78.8 5.0 %collective-permute-start.2 = (f32[1,2,4,9,530]{4,2,1,3,0:T(4,128)S(1)}, f32[1,2,4,9,530]{4,2,1,3,0:T(4,128)S(1)}, u32[]{:S(2)}, u32[]{:S(2)}) collective-permute-start(f32[1,2,4,9,530]{4,2,1,3,0:T(4,128)S(1)} %get-tuple-element.264), channel_id=1, source_target_pairs={{1,0},{2,1},{3,2},{4,3},{5,4},{6,5},{7,6},{8,7},{9,8},{10,9},{11,1... | collective-permute-start | bytes 457928 | tf_op jit(solution)/shard_map/while/body/eval_jaxpr/ppermute | solution.py:18
  80.8 7.8 %collective-permute-start.3 = (f32[1,2,4,9,530]{4,2,1,3,0:T(4,128)S(1)}, f32[1,2,4,9,530]{4,2,1,3,0:T(4,128)S(1)}, u32[]{:S(2)}, u32[]{:S(2)}) collective-permute-start(f32[1,2,4,9,530]{4,2,1,3,0:T(4,128)S(1)} %get-tuple-element.265), channel_id=1, source_target_pairs={{0,1},{1,2},{2,3},{3,4},{4,5},{5,6},{6,7},{7,8},{8,9},{9,10},{10,1... | collective-permute-start | bytes 457928 | tf_op jit(solution)/shard_map/while/body/eval_jaxpr/ppermute | solution.py:17
where the time goes:
time: 131 us
  other arithmetic  73.3 us (56%)
  starting transfers between devices  23.6 us (18%)
  waiting for transfers between devices  13.7 us (10%)
  matrix products  7.03 us (5%)
  blocking collectives  6.5 us (5%)
  local copies, waits for them, and re-layouts  5.51 us (4%)
    select_n x18, other arithmetic, clip_domain(): return jnp.where(keep, field, 0.0)  45.4 us
    ppermute x4, starting transfers between devices, extended(): before = lax.ppermute(last, axis, up)  13.9 us
    ppermute x4, waiting for transfers between devices, extended(): before = lax.ppermute(last, axis, up)  9.45 us
    dot_general x20, matrix products, coefficients(): jnp.einsum('cij,fcp->fpij', onehot, table_part[:, :, :, degree], precisio...  7.03 us
    all_to_all x1, blocking collectives, body(): lax.all_to_all(image, 'depth', split_axis=0, concat_axis=2, tiled=True)  6.5 us
    ppermute x4, starting transfers between devices, extended(): after = lax.ppermute(initial, axis, down)  6.43 us
    add x2, other arithmetic, weigh(): result[:, 2] + (real_part * field[:, 2] + imag_part * field[:, 3])  6.11 us
    add x2, other arithmetic, weigh(): result[:, 3] + (real_part * field[:, 3] - imag_part * field[:, 2])  6.09 us
  transfers between devices with their start and end apart: 9, of which 5 were waited for; matrix products, arithmetic and copies ran while one was open for 6% of the time, Pallas kernels for 0%

commit v1 on v0

--- a/solution.py
+++ b/solution.py
@@ -1,10 +1,17 @@
+import functools
+
 import jax
 import jax.numpy as jnp
 from jax import lax
+from jax.experimental import pallas as pl
+from jax.experimental.pallas import tpu as pltpu
 from jax.sharding import PartitionSpec as P
 
 PASSES = 9
 CLASSES = 8
+LANES = 128
+SUBLANES = 8
+MESH = pl.DeviceIdType.MESH
 
 
 def extended(shard, sides, width):
@@ -130,7 +137,320 @@
     return lax.all_to_all(image, "depth", split_axis=0, concat_axis=2, tiled=True)
 
 
+def chunk_of(count):
+    for rows in (8, 9, 10, 7, 11, 6, 5, 12, 13, 4, 3, 2):
+        if count % rows == 0:
+            return rows
+    return 1
+
+
+def column_sum(field, lane):
+    tiles = [field[..., i : i + LANES] for i in range(0, field.shape[-1], LANES)]
+    turned = [pltpu.roll(t, 1, axis=2) for t in tiles]
+    first = lane == 0
+    pairs = []
+    for i, t in enumerate(tiles):
+        before = turned[i - 1] if i else jnp.zeros_like(t)
+        pairs.append(t + jnp.where(first, before, turned[i]))
+    turned = [pltpu.roll(p, LANES - 1, axis=2) for p in pairs]
+    last = lane == LANES - 1
+    sums = []
+    for i, p in enumerate(pairs):
+        after = turned[i + 1] if i + 1 < len(pairs) else tiles[i]
+        sums.append(p + jnp.where(last, after, turned[i]))
+    return jnp.concatenate(sums, axis=-1)
+
+
+def migrate(
+    strips,
+    surface_ref,
+    velocity_ref,
+    table_ref,
+    image_ref,
+    base,
+    terms,
+    paired,
+    classes,
+    coef,
+    part,
+    rim_send,
+    rim_recv,
+    swap_send,
+    swap_recv,
+):
+    rows, full = velocity_ref.shape
+    width = base.shape[-1]
+    tile = full // 2
+    rim = PASSES
+    tall = rows + 2 * rim
+    step = lax.axis_index("depth")
+    strip = lax.axis_index("strip")
+    other = 1 - step
+    has_up = strip > 0
+    has_down = strip < strips - 1
+    lane_row = lax.broadcasted_iota(jnp.int32, (SUBLANES, LANES), 1)
+    sub = lax.broadcasted_iota(jnp.int32, (SUBLANES, LANES), 0)
+
+    barrier = pltpu.get_barrier_semaphore()
+    pl.semaphore_signal(barrier, inc=1, device_id={"depth": other}, device_id_type=MESH)
+
+    @pl.when(has_up)
+    def _():
+        pl.semaphore_signal(barrier, inc=1, device_id={"strip": strip - 1}, device_id_type=MESH)
+
+    @pl.when(has_down)
+    def _():
+        pl.semaphore_signal(barrier, inc=1, device_id={"strip": strip + 1}, device_id_type=MESH)
+
+    def window(owner):
+        return pl.ds(pl.multiple_of(owner * (full - width), LANES), width)
+
+    for r in range(0, rows, SUBLANES):
+        base[0, pl.ds(rim + r, SUBLANES)] = jnp.swapaxes(
+            surface_ref[:, pl.ds(r, SUBLANES), window(step)], 0, 1
+        )
+
+    pl.semaphore_wait(barrier, 1 + has_up.astype(jnp.int32) + has_down.astype(jnp.int32))
+
+    def rims(level):
+        up = pltpu.make_async_remote_copy(
+            src_ref=base.at[level, pl.ds(rim, rim)],
+            dst_ref=base.at[level, pl.ds(rim + rows, rim)],
+            send_sem=rim_send.at[level, 0],
+            recv_sem=rim_recv.at[level, 0],
+            device_id={"strip": strip - 1},
+            device_id_type=MESH,
+        )
+        down = pltpu.make_async_remote_copy(
+            src_ref=base.at[level, pl.ds(rows, rim)],
+            dst_ref=base.at[level, pl.ds(0, rim)],
+            send_sem=rim_send.at[level, 1],
+            recv_sem=rim_recv.at[level, 1],
+            device_id={"strip": strip + 1},
+            device_id_type=MESH,
+        )
+        return up, down
+
+    def start_rims(level):
+        up, down = rims(level)
+        pl.when(has_up)(up.start)
+        pl.when(has_down)(down.start)
+
+    def zero_rims(level):
+        @pl.when(jnp.logical_not(has_up))
+        def _():
+            base[level, pl.ds(0, rim)] = jnp.zeros((rim, SUBLANES, width), jnp.float32)
+
+        @pl.when(jnp.logical_not(has_down))
+        def _():
+            base[level, pl.ds(rim + rows, rim)] = jnp.zeros((rim, SUBLANES, width), jnp.float32)
+
+    def await_rims(level):
+        up, down = rims(level)
+        pl.when(has_down)(up.wait_recv)
+        pl.when(has_up)(down.wait_recv)
+
+    def end_rims(level):
+        up, down = rims(level)
+        pl.when(has_up)(up.wait_send)
+        pl.when(has_down)(down.wait_send)
+
+    start_rims(0)
+    swap_classes = pltpu.make_async_remote_copy(
+        src_ref=velocity_ref.at[:, window(other)],
+        dst_ref=classes.at[step],
+        send_sem=swap_send.at[0],
+        recv_sem=swap_recv.at[0],
+        device_id={"depth": other},
+        device_id_type=MESH,
+    )
+    swap_classes.start()
+    classes[step] = velocity_ref[:, window(step)]
+    zero_rims(0)
+
+    low_half = sub < SUBLANES // 2
+    quarter = lax.rem(sub, 4)
+    sign = jnp.where((quarter == 1) | (quarter == 2), -1.0, 1.0)
+
+    def fill(degree, carry):
+        for p in range(2):
+            spread = jnp.zeros((SUBLANES, LANES), jnp.float32)
+            for c in range(CLASSES):
+                value = jnp.where(low_half, table_ref[0, c, p, degree], table_ref[1, c, p, degree])
+                spread = jnp.where(lane_row == c, value, spread)
+            coef[p, degree] = spread * sign if p else spread
+        return carry
+
+    lax.fori_loop(0, PASSES + 1, fill, 0)
+
+    swap_classes.wait_recv()
+    tiles = range(0, width, LANES)
+
+    def weigh_row(level, r):
+        kind = classes[level, pl.ds(r, 1), :]
+        swapped = lax.rem(sub, 2) == 0
+        out = []
+        for i in tiles:
+            index = jnp.broadcast_to(kind[:, i : i + LANES], (SUBLANES, LANES))
+            same = cross = None
+            for k in range(PASSES + 1):
+                if k == 0:
+                    term = base[level, rim + r, :, i : i + LANES]
+                else:
+                    term = terms[k - 1, rim + r, :, i : i + LANES]
+                real = jnp.take_along_axis(coef[0, k], index, axis=1) * term
+                imag = jnp.take_along_axis(coef[1, k], index, axis=1) * term
+                same = real if same is None else same + real
+                cross = imag if cross is None else cross + imag
+            cross = jnp.where(
+                swapped, pltpu.roll(cross, SUBLANES - 1, axis=0), pltpu.roll(cross, 1, axis=0)
+            )
+            out.append(same + cross)
+        return jnp.concatenate(out, axis=-1)
+
+    def image_row(level, value, r):
+        kept = lax.rem(lax.broadcasted_iota(jnp.int32, value.shape, 0), 4) >= 2
+        product = jnp.where(kept, value * pltpu.roll(value, 2, axis=0), 0.0)
+        part[level, pl.ds(r, 1), :] = jnp.sum(product, axis=0, keepdims=True)
+
+    for level in range(2):
+        await_rims(level)
+        for degree in range(1, PASSES + 1):
+            count = tall - 2 * degree
+            chunk = chunk_of(count)
+
+            def advance(i, carry, degree=degree, chunk=chunk):
+                at = degree + i * chunk
+                if degree == 1:
+                    field = base[level, pl.ds(at - 1, chunk + 2)]
+                else:
+                    field = terms[degree - 2, pl.ds(at - 1, chunk + 2)]
+                pair = field[:-1] + field[1:]
+                lane = lax.broadcasted_iota(jnp.int32, (chunk, SUBLANES, LANES), 2)
+                spread = column_sum(pair[:-1] + pair[1:], lane)
+                if degree == 1:
+                    joint = 0.125 * spread
+                else:
+                    joint = 0.25 * spread - paired[pl.ds(at, chunk)]
+                if degree < PASSES:
+                    paired[pl.ds(at, chunk)] = joint
+                terms[degree - 1, pl.ds(at, chunk)] = joint - field[1:-1]
+                return carry
+
+            lax.fori_loop(0, count // chunk, advance, 0)
+            if degree < PASSES:
+
+                @pl.when(jnp.logical_not(has_up))
+                def _():
+                    terms[degree - 1, rim - 1] = jnp.zeros((SUBLANES, width), jnp.float32)
+
+                @pl.when(jnp.logical_not(has_down))
+                def _():
+                    terms[degree - 1, rim + rows] = jnp.zeros((SUBLANES, width), jnp.float32)
+
+        def weigh(r, carry):
+            value = weigh_row(level, r)
+            if level == 0:
+                base[1, rim + r] = value
+            image_row(level, value, r)
+            return carry
+
+        lax.fori_loop(0, rows, weigh, 0)
+        if level == 0:
+            start_rims(1)
+            zero_rims(1)
+        here = pl.ds(pl.multiple_of(step * tile, LANES), tile)
+        inner = pl.ds(pl.multiple_of(step * (width - tile), LANES), tile)
+
+        @pl.when(step == level)
+        def _():
+            image_ref[:, here] = part[level, :, inner]
+
+        @pl.when(step != level)
+        def _():
+            pltpu.make_async_remote_copy(
+                src_ref=part.at[level, :, inner],
+                dst_ref=image_ref.at[:, here],
+                send_sem=swap_send.at[1],
+                recv_sem=swap_recv.at[1],
+                device_id={"depth": other},
+                device_id_type=MESH,
+            ).start()
+
+    there = pl.ds(pl.multiple_of(other * tile, LANES), tile)
+    inner = pl.ds(pl.multiple_of(step * (width - tile), LANES), tile)
+    swap_image = pltpu.make_async_remote_copy(
+        src_ref=part.at[0, :, inner],
+        dst_ref=image_ref.at[:, there],
+        send_sem=swap_send.at[1],
+        recv_sem=swap_recv.at[1],
+        device_id={"depth": other},
+        device_id_type=MESH,
+    )
+    swap_image.wait_recv()
+    swap_image.wait_send()
+    swap_classes.wait_send()
+    end_rims(0)
+    end_rims(1)
+
+
+def in_kernel(strips, surface, velocity_class, table):
+    freqs, parts, rows, full = surface.shape
+    width = full // 2 + LANES
+    tall = rows + 2 * PASSES
+    f32 = jnp.float32
+    return pl.pallas_call(
+        functools.partial(migrate, strips),
+        out_shape=jax.ShapeDtypeStruct((rows, full), f32),
+        in_specs=[
+            pl.BlockSpec(memory_space=pltpu.VMEM),
+            pl.BlockSpec(memory_space=pltpu.VMEM),
+            pl.BlockSpec(memory_space=pltpu.SMEM),
+        ],
+        out_specs=pl.BlockSpec(memory_space=pltpu.VMEM),
+        scratch_shapes=[
+            pltpu.VMEM((2, tall, SUBLANES, width), f32),
+            pltpu.VMEM((PASSES, tall, SUBLANES, width), f32),
+            pltpu.VMEM((tall, SUBLANES, width), f32),
+            pltpu.VMEM((2, rows, width), jnp.int32),
+            pltpu.VMEM((2, PASSES + 1, SUBLANES, LANES), f32),
+            pltpu.VMEM((2, rows, width), f32),
+            pltpu.SemaphoreType.DMA((2, 2)),
+            pltpu.SemaphoreType.DMA((2, 2)),
+            pltpu.SemaphoreType.DMA((2,)),
+            pltpu.SemaphoreType.DMA((2,)),
+        ],
+        compiler_params=pltpu.CompilerParams(
+            collective_id=0, has_side_effects=True, vmem_limit_bytes=40 * 2**20
+        ),
+    )(
+        surface.reshape(freqs * parts, rows, full),
+        velocity_class.reshape(rows, full),
+        table,
+    )[None]
+
+
+def fits(mesh, surface, velocity_class):
+    freqs, parts, rows, full = surface.shape
+    return (
+        mesh.shape["depth"] == 2
+        and velocity_class.shape[0] == 1
+        and freqs * parts == SUBLANES
+        and rows % SUBLANES == 0
+        and rows >= PASSES
+        and full % (2 * LANES) == 0
+        and 2 * PASSES <= LANES <= full // 2
+        and rows * full <= 2**15
+    )
+
+
 def solution(mesh):
     in_specs = (P(None, None, "strip", None), P("depth", "strip", None), P())
     out_specs = P("depth", "strip", None)
-    return jax.shard_map(body, mesh=mesh, in_specs=in_specs, out_specs=out_specs, check_vma=False)
+
+    def part(surface, velocity_class, table):
+        if fits(mesh, surface, velocity_class):
+            return in_kernel(mesh.shape["strip"], surface, velocity_class, table)
+        return body(surface, velocity_class, table)
+
+    return jax.shard_map(part, mesh=mesh, in_specs=in_specs, out_specs=out_specs, check_vma=False)

time: 131 us -> 36.8 us (0.28)
  the two profiles are of different devices: /device:TPU:16 before, /device:TPU:14 now
where the time goes in v1:
time: 36.8 us; the launch traced here: 36.5 us
  Pallas kernels  33.3 us (90%)
  local copies, waits for them, and re-layouts  3.23 us (9%)
    pallas_call x1, Pallas kernels, in_kernel(): pl.pallas_call(functools.partial(migrate, strips), out_shape=jax.ShapeDty...  33.3 us
    unnamed x7, local copies, waits for them, and re-layouts  3.23 us

profile of v1, /device:TPU:14, one launch (start us, length us, event | category | flops | bytes accessed | tf_op | source)
XLA Modules:
  0.0 36.5 jit_solution(14255651579454753637)
XLA Ops:
  0.0 0.0 copy-start
  0.0 1.0 %copy-done = f32[2,4,16,1024]{3,2,1,0:T(8,128)S(1)} copy-done((f32[2,4,16,1024]{3,2,1,0:T(8,128)S(1)}, f32[2,4,16,1024]{3,2,1,0:T(8,128)}, u32[]{:S(2)}) %copy-start) | copy-done | bytes 524312
  1.0 0.0 copy-start.1
  1.0 0.8 %copy-done.1 = s32[1,16,1024]{2,1,0:T(8,128)S(1)} copy-done((s32[1,16,1024]{2,1,0:T(8,128)S(1)}, s32[1,16,1024]{2,1,0:T(8,128)}, u32[]{:S(2)}) %copy-start.1) | copy-done | bytes 65560
  1.9 0.0 copy-start.2
  1.9 0.7 %copy-done.2 = f32[2,8,2,10]{3,2,1,0:T(2,128)S(1)} copy-done((f32[2,8,2,10]{3,2,1,0:T(2,128)S(1)}, f32[2,8,2,10]{3,2,1,0:T(2,128)}, u32[]{:S(2)}) %copy-start.2) | copy-done | bytes 1304
  2.6 33.3 %shard_map.37 = f32[16,1024]{1,0:T(8,128)S(1)} custom-call(f32[8,16,1024]{2,1,0:T(8,128)S(1)} %bitcast.3, s32[16,1024]{1,0:T(8,128)S(1)} %bitcast.5, f32[2,8,2,10]{3,2,1,0:T(2,128)S(1)} %copy-done.2), custom_call_target="tpu_custom_call" | custom-call | tf_op jit(solution)/shard_map/pallas_call | solution.py:402
  35.9 0.6 %copy.5 = f32[1,16,1024]{2,1,0:T(8,128)} copy(f32[1,16,1024]{2,1,0:T(8,128)S(1)} %bitcast.4) | data formatting | bytes 131072
Async XLA Ops:
  0.0 1.0 %copy-start = (f32[2,4,16,1024]{3,2,1,0:T(8,128)S(1)}, f32[2,4,16,1024]{3,2,1,0:T(8,128)}, u32[]{:S(2)}) copy-start(f32[2,4,16,1024]{3,2,1,0:T(8,128)} %param.3) | copy-start | bytes 1572868
  1.0 0.8 %copy-start.1 = (s32[1,16,1024]{2,1,0:T(8,128)S(1)}, s32[1,16,1024]{2,1,0:T(8,128)}, u32[]{:S(2)}) copy-start(s32[1,16,1024]{2,1,0:T(8,128)} %param.4) | copy-start | bytes 196612
  1.9 0.7 %copy-start.2 = (f32[2,8,2,10]{3,2,1,0:T(2,128)S(1)}, f32[2,8,2,10]{3,2,1,0:T(2,128)}, u32[]{:S(2)}) copy-start(f32[2,8,2,10]{3,2,1,0:T(2,128)} %table_ref.1) | copy-start | bytes 3844

commit v2 on v0

--- a/solution.py
+++ b/solution.py
@@ -1,10 +1,17 @@
+import functools
+
 import jax
 import jax.numpy as jnp
 from jax import lax
+from jax.experimental import pallas as pl
+from jax.experimental.pallas import tpu as pltpu
 from jax.sharding import PartitionSpec as P
 
 PASSES = 9
 CLASSES = 8
+LANES = 128
+SUBLANES = 8
+MESH = pl.DeviceIdType.MESH
 
 
 def extended(shard, sides, width):
@@ -130,7 +137,339 @@
     return lax.all_to_all(image, "depth", split_axis=0, concat_axis=2, tiled=True)
 
 
+def column_sum(tiles, lane, sub):
+    lower = sub < SUBLANES // 2
+    turned = [pltpu.roll(t, 1, axis=2) for t in tiles]
+    before = jnp.where(lower, 0.0, pltpu.roll(turned[-1], SUBLANES // 2, axis=1))
+    pairs = []
+    for t, now in zip(tiles, turned):
+        pairs.append(t + jnp.where(lane == 0, before, now))
+        before = now
+    turned = [pltpu.roll(p, LANES - 1, axis=2) for p in pairs]
+    after = jnp.where(lower, pltpu.roll(turned[0], SUBLANES // 2, axis=1), tiles[-1])
+    sums = []
+    for p, now in zip(pairs[::-1], turned[::-1]):
+        sums.append(p + jnp.where(lane == LANES - 1, after, now))
+        after = now
+    return sums[::-1]
+
+
+def migrate(strips, surface_ref, velocity_ref, table_ref, image_ref, *scratch):
+    raw, classes, numbers, coef, spot, part, got, paired = scratch[:8]
+    terms = scratch[8 : 9 + PASSES]
+    second = scratch[9 + PASSES]
+    load_sem, rim_send, rim_recv, swap_send, swap_recv = scratch[10 + PASSES :]
+    levels = ((terms[0],) + terms[1:], (second,) + terms[1:])
+    results = (second, paired)
+    rows, full = velocity_ref.shape
+    half = full // 2
+    rim = PASSES
+    tall = rows + 2 * rim
+    step = lax.axis_index("depth")
+    strip = lax.axis_index("strip")
+    other = 1 - step
+    has_up = strip > 0
+    has_down = strip < strips - 1
+    no_up = jnp.logical_not(has_up)
+    no_down = jnp.logical_not(has_down)
+    lane = lax.broadcasted_iota(jnp.int32, (SUBLANES, LANES), 1)
+    sub = lax.broadcasted_iota(jnp.int32, (SUBLANES, LANES), 0)
+    tiles = range(0, half, LANES)
+
+    load_surface = pltpu.make_async_copy(surface_ref.at[step], raw, load_sem.at[0])
+    load_classes = pltpu.make_async_copy(velocity_ref, classes.at[step], load_sem.at[1])
+    load_table = pltpu.make_async_copy(table_ref, numbers, load_sem.at[2])
+    load_surface.start()
+    load_classes.start()
+    load_table.start()
+
+    barrier = pltpu.get_barrier_semaphore()
+    pl.semaphore_signal(barrier, inc=1, device_id={"depth": other}, device_id_type=MESH)
+
+    @pl.when(has_up)
+    def _():
+        pl.semaphore_signal(barrier, inc=1, device_id={"strip": strip - 1}, device_id_type=MESH)
+
+    @pl.when(has_down)
+    def _():
+        pl.semaphore_signal(barrier, inc=1, device_id={"strip": strip + 1}, device_id_type=MESH)
+
+    load_surface.wait()
+    for r in range(0, rows, SUBLANES):
+        for i in tiles:
+            block = jnp.concatenate(
+                [raw[:, r : r + SUBLANES, i : i + LANES], raw[:, r : r + SUBLANES, half + i : half + i + LANES]],
+                axis=0,
+            )
+            terms[0][rim + r : rim + r + SUBLANES, :, i : i + LANES] = jnp.swapaxes(block, 0, 1)
+
+    load_classes.wait()
+    pl.semaphore_wait(barrier, 1 + has_up.astype(jnp.int32) + has_down.astype(jnp.int32))
+
+    def rims(level):
+        base = levels[level][0]
+        up = pltpu.make_async_remote_copy(
+            src_ref=base.at[pl.ds(rim, rim)],
+            dst_ref=base.at[pl.ds(rim + rows, rim)],
+            send_sem=rim_send.at[level, 0],
+            recv_sem=rim_recv.at[level, 0],
+            device_id={"strip": strip - 1},
+            device_id_type=MESH,
+        )
+        down = pltpu.make_async_remote_copy(
+            src_ref=base.at[pl.ds(rows, rim)],
+            dst_ref=base.at[pl.ds(0, rim)],
+            send_sem=rim_send.at[level, 1],
+            recv_sem=rim_recv.at[level, 1],
+            device_id={"strip": strip + 1},
+            device_id_type=MESH,
+        )
+        return up, down
+
+    def start_rims(level):
+        up, down = rims(level)
+        pl.when(has_up)(up.start)
+        pl.when(has_down)(down.start)
+
+    def zero_rims(level):
+        base = levels[level][0]
+
+        @pl.when(no_up)
+        def _():
+            base[:rim] = jnp.zeros((rim, SUBLANES, half), jnp.float32)
+
+        @pl.when(no_down)
+        def _():
+            base[rim + rows :] = jnp.zeros((rim, SUBLANES, half), jnp.float32)
+
+    def swap_image(level):
+        return pltpu.make_async_remote_copy(
+            src_ref=part.at[level],
+            dst_ref=got,
+            send_sem=swap_send.at[1],
+            recv_sem=swap_recv.at[1],
+            device_id={"depth": other},
+            device_id_type=MESH,
+        )
+
+    start_rims(0)
+    swap_classes = pltpu.make_async_remote_copy(
+        src_ref=classes.at[step],
+        dst_ref=classes.at[step],
+        send_sem=swap_send.at[0],
+        recv_sem=swap_recv.at[0],
+        device_id={"depth": other},
+        device_id_type=MESH,
+    )
+    swap_classes.start()
+    zero_rims(0)
+
+    quarter = lax.rem(sub, 4)
+    sign = jnp.where((quarter == 1) | (quarter == 2), -1.0, 1.0)
+    load_table.wait()
+
+    def fill(degree, carry):
+        for p in range(2):
+            spread = jnp.zeros((SUBLANES, LANES), jnp.float32)
+            for c in range(CLASSES):
+                spread = jnp.where(lane == c, numbers[step, c, p, degree], spread)
+            coef[p, degree] = spread * sign if p else spread
+        return carry
+
+    lax.fori_loop(0, PASSES + 1, fill, 0)
+
+    def look_up(level):
+        def row(r, carry):
+            kind = classes[level, pl.ds(r, 1), :]
+            for i in tiles:
+                index = jnp.where(
+                    sub < SUBLANES // 2,
+                    jnp.broadcast_to(kind[:, i : i + LANES], (SUBLANES, LANES)),
+                    jnp.broadcast_to(kind[:, half + i : half + i + LANES], (SUBLANES, LANES)),
+                )
+                for p in range(2):
+                    for k in range(PASSES + 1):
+                        spot[p, k, r, :, i : i + LANES] = jnp.take_along_axis(coef[p, k], index, axis=1)
+            return carry
+
+        lax.fori_loop(0, rows, row, 0)
+
+    def weigh(level, low, high):
+        held = levels[level]
+        even = lax.rem(sub, 2) == 0
+
+        def row(r, carry):
+            for i in tiles:
+                same = cross = None
+                for k in range(PASSES + 1):
+                    term = held[k][rim + r, :, i : i + LANES]
+                    real = spot[0, k, r, :, i : i + LANES] * term
+                    imag = spot[1, k, r, :, i : i + LANES] * term
+                    same = real if same is None else same + real
+                    cross = imag if cross is None else cross + imag
+                cross = jnp.where(
+                    even, pltpu.roll(cross, SUBLANES - 1, axis=0), pltpu.roll(cross, 1, axis=0)
+                )
+                results[level][rim + r, :, i : i + LANES] = same + cross
+            return carry
+
+        lax.fori_loop(low, high, row, 0)
+
+    def correlate_step(level):
+        for r in range(0, rows, SUBLANES):
+            for i in tiles:
+                field = results[level][rim + r : rim + r + SUBLANES, :, i : i + LANES]
+                field = jnp.swapaxes(field, 0, 1)
+                part[level, r : r + SUBLANES, i : i + LANES] = field[0] * field[2] + field[1] * field[3]
+                part[level, r : r + SUBLANES, half + i : half + i + LANES] = (
+                    field[4] * field[6] + field[5] * field[7]
+                )
+
+    def sweep(level, degree, low, high):
+        source, target = levels[level][degree - 1], levels[level][degree]
+        at = low
+        while at < high:
+            size = min(3, high - at)
+            if high - at == 4:
+                size = 2
+            lanes = lax.broadcasted_iota(jnp.int32, (size, SUBLANES, LANES), 2)
+            subs = lax.broadcasted_iota(jnp.int32, (size, SUBLANES, LANES), 1)
+            sums = []
+            inner = []
+            for i in tiles:
+                field = source[at - 1 : at + size + 1, :, i : i + LANES]
+                pair = field[:-1] + field[1:]
+                sums.append(pair[:-1] + pair[1:])
+                inner.append(field[1:-1])
+            for i, total, field in zip(tiles, column_sum(sums, lanes, subs), inner):
+                if degree == 1:
+                    joint = 0.125 * total
+                else:
+                    joint = 0.25 * total - paired[at : at + size, :, i : i + LANES]
+                if degree < PASSES:
+                    paired[at : at + size, :, i : i + LANES] = joint
+                target[at : at + size, :, i : i + LANES] = joint - field
+            at += size
+
+    def inside(level):
+        for degree in range(1, PASSES):
+            low, high = rim + degree, rim + rows - degree
+            if low < high:
+                sweep(level, degree, low, high)
+
+    def above(level):
+        for degree in range(1, PASSES):
+            sweep(level, degree, degree, min(rim + degree, tall // 2))
+            @pl.when(no_up)
+            def _():
+                levels[level][degree][rim - 1] = jnp.zeros((SUBLANES, half), jnp.float32)
+
+    def below(level):
+        for degree in range(1, PASSES):
+            sweep(level, degree, max(rim + rows - degree, tall // 2), tall - degree)
+            @pl.when(no_down)
+            def _():
+                levels[level][degree][rim + rows] = jnp.zeros((SUBLANES, half), jnp.float32)
+
+    for level in range(2):
+        if level == 0:
+            swap_classes.wait_recv()
+        inside(level)
+        look_up(level)
+        if level == 1:
+            correlate_step(0)
+
+            @pl.when(step == 1)
+            def _():
+                swap_image(0).start()
+
+        up, down = rims(level)
+        pl.when(has_up)(down.wait_recv)
+        above(level)
+        pl.when(has_down)(up.wait_recv)
+        below(level)
+        sweep(level, PASSES, rim, rim + rows)
+        if level == 0:
+            up, down = rims(1)
+            weigh(0, 0, rim)
+            pl.when(has_up)(up.start)
+            weigh(0, rim, rows)
+            pl.when(has_down)(down.start)
+            zero_rims(1)
+        else:
+            weigh(1, 0, rows)
+            correlate_step(1)
+
+    @pl.when(step == 0)
+    def _():
+        swap_image(1).start()
+
+    swap = swap_image(0)
+    swap.wait_recv()
+    image_ref[...] = part[step] + got[...]
+    swap.wait_send()
+    swap_classes.wait_send()
+    for level in range(2):
+        up, down = rims(level)
+        pl.when(has_up)(up.wait_send)
+        pl.when(has_down)(down.wait_send)
+
+
+def in_kernel(strips, surface, velocity_class, table):
+    freqs, parts, rows, full = surface.shape
+    half = full // 2
+    tall = rows + 2 * PASSES
+    f32 = jnp.float32
+    fields = pltpu.VMEM((tall, SUBLANES, half), f32)
+    return pl.pallas_call(
+        functools.partial(migrate, strips),
+        out_shape=jax.ShapeDtypeStruct((rows, full), f32),
+        in_specs=[pl.BlockSpec(memory_space=pl.ANY)] * 3,
+        out_specs=pl.BlockSpec(memory_space=pltpu.VMEM),
+        scratch_shapes=[
+            pltpu.VMEM((parts, rows, full), f32),
+            pltpu.VMEM((2, rows, full), jnp.int32),
+            pltpu.SMEM(table.shape, f32),
+            pltpu.VMEM((2, PASSES + 1, SUBLANES, LANES), f32),
+            pltpu.VMEM((2, PASSES + 1, rows, SUBLANES, half), f32),
+            pltpu.VMEM((2, rows, full), f32),
+            pltpu.VMEM((rows, full), f32),
+        ]
+        + [fields] * (PASSES + 3)
+        + [
+            pltpu.SemaphoreType.DMA((3,)),
+            pltpu.SemaphoreType.DMA((2, 2)),
+            pltpu.SemaphoreType.DMA((2, 2)),
+            pltpu.SemaphoreType.DMA((2,)),
+            pltpu.SemaphoreType.DMA((2,)),
+        ],
+        compiler_params=pltpu.CompilerParams(
+            collective_id=0, has_side_effects=True, vmem_limit_bytes=56 * 2**20
+        ),
+    )(surface, velocity_class.reshape(rows, full), table)[None]
+
+
+def fits(mesh, surface, velocity_class):
+    freqs, parts, rows, full = surface.shape
+    return (
+        mesh.shape["depth"] == 2
+        and velocity_class.shape[0] == 1
+        and freqs == 2
+        and 2 * parts == SUBLANES
+        and rows % SUBLANES == 0
+        and PASSES <= rows < 2 * PASSES
+        and full % (2 * LANES) == 0
+        and rows * full <= 2**15
+    )
+
+
 def solution(mesh):
     in_specs = (P(None, None, "strip", None), P("depth", "strip", None), P())
     out_specs = P("depth", "strip", None)
-    return jax.shard_map(body, mesh=mesh, in_specs=in_specs, out_specs=out_specs, check_vma=False)
+
+    def part(surface, velocity_class, table):
+        if fits(mesh, surface, velocity_class):
+            return in_kernel(mesh.shape["strip"], surface, velocity_class, table)
+        return body(surface, velocity_class, table)
+
+    return jax.shard_map(part, mesh=mesh, in_specs=in_specs, out_specs=out_specs, check_vma=False)

time: 131 us -> 27.7 us (0.21)
  the two profiles are of different devices: /device:TPU:16 before, /device:TPU:0 now
where the time goes in v2:
time: 27.7 us; the launch traced here: 27.6 us
  Pallas kernels  26.1 us (94%)
  local copies, waits for them, and re-layouts  1.47 us (5%)
    pallas_call x1, Pallas kernels, in_kernel(): pl.pallas_call(functools.partial(migrate, strips), out_shape=jax.ShapeDty...  26.1 us
    unnamed x1, local copies, waits for them, and re-layouts  1.47 us

profile of v2, /device:TPU:0, one launch (start us, length us, event | category | flops | bytes accessed | tf_op | source)
XLA Modules:
  0.0 27.6 jit_solution(9863602145662976018)
XLA Ops:
  0.0 26.1 %shard_map.37 = f32[16,1024]{1,0:T(8,128)} custom-call(f32[2,4,16,1024]{3,2,1,0:T(8,128)} %surface_ref.1, s32[16,1024]{1,0:T(8,128)} %bitcast.3, f32[2,8,2,10]{3,2,1,0:T(2,128)} %table_ref.1), custom_call_target="tpu_custom_call" | custom-call | tf_op jit(solution)/shard_map/pallas_call | solution.py:424
  26.1 1.5 %copy.5 = f32[1,16,1024]{2,1,0:T(8,128)} copy(f32[1,16,1024]{2,1,0:T(8,128)} %bitcast.2) | data formatting | bytes 131072

commit v3 on v2

--- a/solution.py
+++ b/solution.py
@@ -139,19 +139,16 @@
 
 def column_sum(tiles, lane, sub):
     lower = sub < SUBLANES // 2
-    turned = [pltpu.roll(t, 1, axis=2) for t in tiles]
-    before = jnp.where(lower, 0.0, pltpu.roll(turned[-1], SUBLANES // 2, axis=1))
-    pairs = []
-    for t, now in zip(tiles, turned):
-        pairs.append(t + jnp.where(lane == 0, before, now))
-        before = now
-    turned = [pltpu.roll(p, LANES - 1, axis=2) for p in pairs]
-    after = jnp.where(lower, pltpu.roll(turned[0], SUBLANES // 2, axis=1), tiles[-1])
+    rights = [pltpu.roll(t, 1, axis=2) for t in tiles]
+    lefts = [pltpu.roll(t, LANES - 1, axis=2) for t in tiles]
+    before = jnp.where(lower, 0.0, pltpu.roll(rights[-1], SUBLANES // 2, axis=1))
+    after = jnp.where(lower, pltpu.roll(lefts[0], SUBLANES // 2, axis=1), 0.0)
     sums = []
-    for p, now in zip(pairs[::-1], turned[::-1]):
-        sums.append(p + jnp.where(lane == LANES - 1, after, now))
-        after = now
-    return sums[::-1]
+    for i, t in enumerate(tiles):
+        right = jnp.where(lane == 0, rights[i - 1] if i else before, rights[i])
+        left = jnp.where(lane == LANES - 1, lefts[i + 1] if i + 1 < len(tiles) else after, lefts[i])
+        sums.append((right + left) + (t + t))
+    return sums
 
 
 def migrate(strips, surface_ref, velocity_ref, table_ref, image_ref, *scratch):
@@ -242,12 +239,13 @@
         def _():
             base[rim + rows :] = jnp.zeros((rim, SUBLANES, half), jnp.float32)
 
-    def swap_image(level):
+    def swap_image(level, piece):
+        here = pl.ds(piece * (rows // 2), rows // 2)
         return pltpu.make_async_remote_copy(
-            src_ref=part.at[level],
-            dst_ref=got,
-            send_sem=swap_send.at[1],
-            recv_sem=swap_recv.at[1],
+            src_ref=part.at[level, here],
+            dst_ref=got.at[here],
+            send_sem=swap_send.at[1 + piece],
+            recv_sem=swap_recv.at[1 + piece],
             device_id={"depth": other},
             device_id_type=MESH,
         )
@@ -279,44 +277,45 @@
     lax.fori_loop(0, PASSES + 1, fill, 0)
 
     def look_up(level):
-        def row(r, carry):
-            kind = classes[level, pl.ds(r, 1), :]
-            for i in tiles:
-                index = jnp.where(
-                    sub < SUBLANES // 2,
-                    jnp.broadcast_to(kind[:, i : i + LANES], (SUBLANES, LANES)),
-                    jnp.broadcast_to(kind[:, half + i : half + i + LANES], (SUBLANES, LANES)),
-                )
-                for p in range(2):
-                    for k in range(PASSES + 1):
-                        spot[p, k, r, :, i : i + LANES] = jnp.take_along_axis(coef[p, k], index, axis=1)
+        def block(b, carry):
+            for j in range(4):
+                r = b * 4 + j
+                kind = classes[level, pl.ds(r, 1), :]
+                for i in tiles:
+                    index = jnp.where(
+                        sub < SUBLANES // 2,
+                        jnp.broadcast_to(kind[:, i : i + LANES], (SUBLANES, LANES)),
+                        jnp.broadcast_to(kind[:, half + i : half + i + LANES], (SUBLANES, LANES)),
+                    )
+                    for p in range(2):
+                        for k in range(PASSES + 1):
+                            spot[p, k, r, :, i : i + LANES] = jnp.take_along_axis(
+                                coef[p, k], index, axis=1, mode="promise_in_bounds"
+                            )
             return carry
 
-        lax.fori_loop(0, rows, row, 0)
+        lax.fori_loop(0, rows // 4, block, 0)
 
     def weigh(level, low, high):
         held = levels[level]
-        even = lax.rem(sub, 2) == 0
-
-        def row(r, carry):
+        for r in range(low, high, 4):
+            size = min(4, high - r)
+            even = lax.rem(lax.broadcasted_iota(jnp.int32, (size, SUBLANES, LANES), 1), 2) == 0
             for i in tiles:
                 same = cross = None
                 for k in range(PASSES + 1):
-                    term = held[k][rim + r, :, i : i + LANES]
-                    real = spot[0, k, r, :, i : i + LANES] * term
-                    imag = spot[1, k, r, :, i : i + LANES] * term
+                    term = held[k][rim + r : rim + r + size, :, i : i + LANES]
+                    real = spot[0, k, r : r + size, :, i : i + LANES] * term
+                    imag = spot[1, k, r : r + size, :, i : i + LANES] * term
                     same = real if same is None else same + real
                     cross = imag if cross is None else cross + imag
                 cross = jnp.where(
-                    even, pltpu.roll(cross, SUBLANES - 1, axis=0), pltpu.roll(cross, 1, axis=0)
+                    even, pltpu.roll(cross, SUBLANES - 1, axis=1), pltpu.roll(cross, 1, axis=1)
                 )
-                results[level][rim + r, :, i : i + LANES] = same + cross
-            return carry
-
-        lax.fori_loop(low, high, row, 0)
-
-    def correlate_step(level):
-        for r in range(0, rows, SUBLANES):
+                results[level][rim + r : rim + r + size, :, i : i + LANES] = same + cross
+
+    def correlate_step(level, low, high):
+        for r in range(low, high, SUBLANES):
             for i in tiles:
                 field = results[level][rim + r : rim + r + SUBLANES, :, i : i + LANES]
                 field = jnp.swapaxes(field, 0, 1)
@@ -325,13 +324,17 @@
                     field[4] * field[6] + field[5] * field[7]
                 )
 
-    def sweep(level, degree, low, high):
+    def groups(low, high):
+        found, at = [], low
+        while at < high:
+            size = 2 if high - at == 4 else min(3, high - at)
+            found.append((at, size))
+            at += size
+        return found
+
+    def sweep(level, degree, spans):
         source, target = levels[level][degree - 1], levels[level][degree]
-        at = low
-        while at < high:
-            size = min(3, high - at)
-            if high - at == 4:
-                size = 2
+        for at, size in spans:
             lanes = lax.broadcasted_iota(jnp.int32, (size, SUBLANES, LANES), 2)
             subs = lax.broadcasted_iota(jnp.int32, (size, SUBLANES, LANES), 1)
             sums = []
@@ -348,47 +351,46 @@
                     joint = 0.25 * total - paired[at : at + size, :, i : i + LANES]
                 if degree < PASSES:
                     paired[at : at + size, :, i : i + LANES] = joint
-                target[at : at + size, :, i : i + LANES] = joint - field
-            at += size
+                value = joint - field
+                for edge, absent in ((rim - 1, no_up), (rim + rows, no_down)):
+                    if at <= edge < at + size:
+                        j = edge - at
+                        lines = [value[row : row + 1] for row in range(size)]
+                        lines[j] = jnp.where(absent, 0.0, lines[j])
+                        value = jnp.concatenate(lines, axis=0)
+                target[at : at + size, :, i : i + LANES] = value
 
     def inside(level):
         for degree in range(1, PASSES):
-            low, high = rim + degree, rim + rows - degree
-            if low < high:
-                sweep(level, degree, low, high)
-
-    def above(level):
+            if rim + degree < rim + rows - degree:
+                sweep(level, degree, groups(rim + degree, rim + rows - degree))
+
+    def outside(level):
+        middle = tall // 2
         for degree in range(1, PASSES):
-            sweep(level, degree, degree, min(rim + degree, tall // 2))
-            @pl.when(no_up)
-            def _():
-                levels[level][degree][rim - 1] = jnp.zeros((SUBLANES, half), jnp.float32)
-
-    def below(level):
-        for degree in range(1, PASSES):
-            sweep(level, degree, max(rim + rows - degree, tall // 2), tall - degree)
-            @pl.when(no_down)
-            def _():
-                levels[level][degree][rim + rows] = jnp.zeros((SUBLANES, half), jnp.float32)
-
+            above = groups(degree, min(rim + degree, middle))
+            below = groups(max(rim + rows - degree, middle), tall - degree)
+            sweep(level, degree, [span for both in zip(above, below) for span in both])
+        sweep(level, PASSES, groups(rim, rim + rows))
+
+    middle = rows // 2
     for level in range(2):
+        inside(level)
         if level == 0:
             swap_classes.wait_recv()
-        inside(level)
         look_up(level)
         if level == 1:
-            correlate_step(0)
+            correlate_step(0, 0, rows)
 
             @pl.when(step == 1)
             def _():
-                swap_image(0).start()
+                swap_image(0, 0).start()
+                swap_image(0, 1).start()
 
         up, down = rims(level)
         pl.when(has_up)(down.wait_recv)
-        above(level)
         pl.when(has_down)(up.wait_recv)
-        below(level)
-        sweep(level, PASSES, rim, rim + rows)
+        outside(level)
         if level == 0:
             up, down = rims(1)
             weigh(0, 0, rim)
@@ -397,17 +399,21 @@
             pl.when(has_down)(down.start)
             zero_rims(1)
         else:
-            weigh(1, 0, rows)
-            correlate_step(1)
-
-    @pl.when(step == 0)
-    def _():
-        swap_image(1).start()
-
-    swap = swap_image(0)
-    swap.wait_recv()
-    image_ref[...] = part[step] + got[...]
-    swap.wait_send()
+            for piece in range(2):
+                weigh(1, piece * middle, (piece + 1) * middle)
+                correlate_step(1, piece * middle, (piece + 1) * middle)
+
+                @pl.when(step == 0)
+                def _(piece=piece):
+                    swap_image(1, piece).start()
+
+    for piece in range(2):
+        swap = swap_image(0, piece)
+        swap.wait_recv()
+        here = pl.ds(piece * middle, middle)
+        image_ref[here] = part[step, here] + got[here]
+    for piece in range(2):
+        swap_image(0, piece).wait_send()
     swap_classes.wait_send()
     for level in range(2):
         up, down = rims(level)
@@ -440,8 +446,8 @@
             pltpu.SemaphoreType.DMA((3,)),
             pltpu.SemaphoreType.DMA((2, 2)),
             pltpu.SemaphoreType.DMA((2, 2)),
-            pltpu.SemaphoreType.DMA((2,)),
-            pltpu.SemaphoreType.DMA((2,)),
+            pltpu.SemaphoreType.DMA((3,)),
+            pltpu.SemaphoreType.DMA((3,)),
         ],
         compiler_params=pltpu.CompilerParams(
             collective_id=0, has_side_effects=True, vmem_limit_bytes=56 * 2**20
@@ -456,7 +462,7 @@
         and velocity_class.shape[0] == 1
         and freqs == 2
         and 2 * parts == SUBLANES
-        and rows % SUBLANES == 0
+        and rows % (2 * SUBLANES) == 0
         and PASSES <= rows < 2 * PASSES
         and full % (2 * LANES) == 0
         and rows * full <= 2**15

time: 27.7 us -> 20.8 us (0.75)
  the two profiles are of different devices: /device:TPU:0 before, /device:TPU:11 now
where the time goes in v3:
time: 20.8 us; the launch traced here: 20.6 us
  Pallas kernels  19.1 us (92%)
  local copies, waits for them, and re-layouts  1.47 us (7%)
    pallas_call x1, Pallas kernels, in_kernel(): pl.pallas_call(functools.partial(migrate, strips), out_shape=jax.ShapeDty...  19.1 us
    unnamed x1, local copies, waits for them, and re-layouts  1.47 us

profile of v3, /device:TPU:11, one launch (start us, length us, event | category | flops | bytes accessed | tf_op | source)
XLA Modules:
  0.0 20.6 jit_solution(14469547781714031935)
XLA Ops:
  0.0 19.1 %shard_map.37 = f32[16,1024]{1,0:T(8,128)} custom-call(f32[2,4,16,1024]{3,2,1,0:T(8,128)} %surface_ref.1, s32[16,1024]{1,0:T(8,128)} %bitcast.3, f32[2,8,2,10]{3,2,1,0:T(2,128)} %table_ref.1), custom_call_target="tpu_custom_call" | custom-call | tf_op jit(solution)/shard_map/pallas_call | solution.py:430
  19.1 1.5 %copy.5 = f32[1,16,1024]{2,1,0:T(8,128)} copy(f32[1,16,1024]{2,1,0:T(8,128)} %bitcast.2) | data formatting | bytes 131072

commit v4 on v3

--- a/solution.py
+++ b/solution.py
@@ -11,6 +11,7 @@
 CLASSES = 8
 LANES = 128
 SUBLANES = 8
+QUARTERS = 4
 MESH = pl.DeviceIdType.MESH
 
 
@@ -138,11 +139,10 @@
 
 
 def column_sum(tiles, lane, sub):
-    lower = sub < SUBLANES // 2
     rights = [pltpu.roll(t, 1, axis=2) for t in tiles]
     lefts = [pltpu.roll(t, LANES - 1, axis=2) for t in tiles]
-    before = jnp.where(lower, 0.0, pltpu.roll(rights[-1], SUBLANES // 2, axis=1))
-    after = jnp.where(lower, pltpu.roll(lefts[0], SUBLANES // 2, axis=1), 0.0)
+    before = jnp.where(sub < 2, 0.0, pltpu.roll(rights[-1], 2, axis=1))
+    after = jnp.where(sub < SUBLANES - 2, pltpu.roll(lefts[0], SUBLANES - 2, axis=1), 0.0)
     sums = []
     for i, t in enumerate(tiles):
         right = jnp.where(lane == 0, rights[i - 1] if i else before, rights[i])
@@ -152,14 +152,20 @@
 
 
 def migrate(strips, surface_ref, velocity_ref, table_ref, image_ref, *scratch):
-    raw, classes, numbers, coef, spot, part, got, paired = scratch[:8]
-    terms = scratch[8 : 9 + PASSES]
-    second = scratch[9 + PASSES]
-    load_sem, rim_send, rim_recv, swap_send, swap_recv = scratch[10 + PASSES :]
-    levels = ((terms[0],) + terms[1:], (second,) + terms[1:])
-    results = (second, paired)
+    raw, classes, numbers, coef, spot, part, got = scratch[:7]
+    per_group = PASSES + 3
+    held = [scratch[7 + g * per_group : 7 + (g + 1) * per_group] for g in range(2)]
+    load_sem, rim_send, rim_recv, swap_send, swap_recv = scratch[7 + 2 * per_group :]
+    first = [h[0] for h in held]
+    second = [h[1] for h in held]
+    paired = [h[2] for h in held]
+    terms = [[[first, second][level][g]] + list(held[g][3:]) for g in range(2) for level in range(2)]
+
+    def term(g, level):
+        return terms[2 * g + level]
+
     rows, full = velocity_ref.shape
-    half = full // 2
+    wide = full // QUARTERS
     rim = PASSES
     tall = rows + 2 * rim
     step = lax.axis_index("depth")
@@ -171,7 +177,7 @@
     no_down = jnp.logical_not(has_down)
     lane = lax.broadcasted_iota(jnp.int32, (SUBLANES, LANES), 1)
     sub = lax.broadcasted_iota(jnp.int32, (SUBLANES, LANES), 0)
-    tiles = range(0, half, LANES)
+    tiles = range(0, wide, LANES)
 
     load_surface = pltpu.make_async_copy(surface_ref.at[step], raw, load_sem.at[0])
     load_classes = pltpu.make_async_copy(velocity_ref, classes.at[step], load_sem.at[1])
@@ -192,52 +198,56 @@
         pl.semaphore_signal(barrier, inc=1, device_id={"strip": strip + 1}, device_id_type=MESH)
 
     load_surface.wait()
-    for r in range(0, rows, SUBLANES):
-        for i in tiles:
-            block = jnp.concatenate(
-                [raw[:, r : r + SUBLANES, i : i + LANES], raw[:, r : r + SUBLANES, half + i : half + i + LANES]],
-                axis=0,
-            )
-            terms[0][rim + r : rim + r + SUBLANES, :, i : i + LANES] = jnp.swapaxes(block, 0, 1)
+    for g in range(2):
+        for r in range(0, rows, SUBLANES):
+            for i in tiles:
+                block = jnp.concatenate(
+                    [
+                        raw[2 * g : 2 * g + 2, r : r + SUBLANES, q * wide + i : q * wide + i + LANES]
+                        for q in range(QUARTERS)
+                    ],
+                    axis=0,
+                )
+                first[g][rim + r : rim + r + SUBLANES, :, i : i + LANES] = jnp.swapaxes(block, 0, 1)
 
     load_classes.wait()
     pl.semaphore_wait(barrier, 1 + has_up.astype(jnp.int32) + has_down.astype(jnp.int32))
 
-    def rims(level):
-        base = levels[level][0]
+    def rims(g, level):
+        base = term(g, level)[0]
         up = pltpu.make_async_remote_copy(
             src_ref=base.at[pl.ds(rim, rim)],
             dst_ref=base.at[pl.ds(rim + rows, rim)],
-            send_sem=rim_send.at[level, 0],
-            recv_sem=rim_recv.at[level, 0],
+            send_sem=rim_send.at[g, level, 0],
+            recv_sem=rim_recv.at[g, level, 0],
             device_id={"strip": strip - 1},
             device_id_type=MESH,
         )
         down = pltpu.make_async_remote_copy(
             src_ref=base.at[pl.ds(rows, rim)],
             dst_ref=base.at[pl.ds(0, rim)],
-            send_sem=rim_send.at[level, 1],
-            recv_sem=rim_recv.at[level, 1],
+            send_sem=rim_send.at[g, level, 1],
+            recv_sem=rim_recv.at[g, level, 1],
             device_id={"strip": strip + 1},
             device_id_type=MESH,
         )
         return up, down
 
-    def start_rims(level):
-        up, down = rims(level)
-        pl.when(has_up)(up.start)
-        pl.when(has_down)(down.start)
+    def await_rims(g, level):
+        up, down = rims(g, level)
+        pl.when(has_up)(down.wait_recv)
+        pl.when(has_down)(up.wait_recv)
 
     def zero_rims(level):
-        base = levels[level][0]
-
         @pl.when(no_up)
         def _():
-            base[:rim] = jnp.zeros((rim, SUBLANES, half), jnp.float32)
+            for g in range(2):
+                term(g, level)[0][:rim] = jnp.zeros((rim, SUBLANES, wide), jnp.float32)
 
         @pl.when(no_down)
         def _():
-            base[rim + rows :] = jnp.zeros((rim, SUBLANES, half), jnp.float32)
+            for g in range(2):
+                term(g, level)[0][rim + rows :] = jnp.zeros((rim, SUBLANES, wide), jnp.float32)
 
     def swap_image(level, piece):
         here = pl.ds(piece * (rows // 2), rows // 2)
@@ -250,7 +260,10 @@
             device_id_type=MESH,
         )
 
-    start_rims(0)
+    for g in range(2):
+        up, down = rims(g, 0)
+        pl.when(has_up)(up.start)
+        pl.when(has_down)(down.start)
     swap_classes = pltpu.make_async_remote_copy(
         src_ref=classes.at[step],
         dst_ref=classes.at[step],
@@ -261,9 +274,9 @@
     )
     swap_classes.start()
     zero_rims(0)
-
-    quarter = lax.rem(sub, 4)
-    sign = jnp.where((quarter == 1) | (quarter == 2), -1.0, 1.0)
+    zero_rims(1)
+
+    sign = jnp.where(lax.rem(sub, 2) == 1, -1.0, 1.0)
     load_table.wait()
 
     def fill(degree, carry):
@@ -282,11 +295,11 @@
                 r = b * 4 + j
                 kind = classes[level, pl.ds(r, 1), :]
                 for i in tiles:
-                    index = jnp.where(
-                        sub < SUBLANES // 2,
-                        jnp.broadcast_to(kind[:, i : i + LANES], (SUBLANES, LANES)),
-                        jnp.broadcast_to(kind[:, half + i : half + i + LANES], (SUBLANES, LANES)),
-                    )
+                    index = None
+                    for q in range(QUARTERS):
+                        at = q * wide + i
+                        spread = jnp.broadcast_to(kind[:, at : at + LANES], (SUBLANES, LANES))
+                        index = spread if q == 0 else jnp.where(sub < 2 * q, index, spread)
                     for p in range(2):
                         for k in range(PASSES + 1):
                             spot[p, k, r, :, i : i + LANES] = jnp.take_along_axis(
@@ -296,44 +309,51 @@
 
         lax.fori_loop(0, rows // 4, block, 0)
 
-    def weigh(level, low, high):
-        held = levels[level]
+    results = (second, paired)
+
+    def weigh(g, level, low, high):
+        series = term(g, level)
         for r in range(low, high, 4):
             size = min(4, high - r)
             even = lax.rem(lax.broadcasted_iota(jnp.int32, (size, SUBLANES, LANES), 1), 2) == 0
             for i in tiles:
                 same = cross = None
                 for k in range(PASSES + 1):
-                    term = held[k][rim + r : rim + r + size, :, i : i + LANES]
-                    real = spot[0, k, r : r + size, :, i : i + LANES] * term
-                    imag = spot[1, k, r : r + size, :, i : i + LANES] * term
+                    field = series[k][rim + r : rim + r + size, :, i : i + LANES]
+                    real = spot[0, k, r : r + size, :, i : i + LANES] * field
+                    imag = spot[1, k, r : r + size, :, i : i + LANES] * field
                     same = real if same is None else same + real
                     cross = imag if cross is None else cross + imag
                 cross = jnp.where(
                     even, pltpu.roll(cross, SUBLANES - 1, axis=1), pltpu.roll(cross, 1, axis=1)
                 )
-                results[level][rim + r : rim + r + size, :, i : i + LANES] = same + cross
+                results[level][g][rim + r : rim + r + size, :, i : i + LANES] = (
+                    same - cross if g else same + cross
+                )
 
     def correlate_step(level, low, high):
         for r in range(low, high, SUBLANES):
             for i in tiles:
-                field = results[level][rim + r : rim + r + SUBLANES, :, i : i + LANES]
-                field = jnp.swapaxes(field, 0, 1)
-                part[level, r : r + SUBLANES, i : i + LANES] = field[0] * field[2] + field[1] * field[3]
-                part[level, r : r + SUBLANES, half + i : half + i + LANES] = (
-                    field[4] * field[6] + field[5] * field[7]
+                source, receiver = (
+                    results[level][g][rim + r : rim + r + SUBLANES, :, i : i + LANES] for g in range(2)
                 )
+                product = jnp.swapaxes(source * receiver, 0, 1)
+                for q in range(QUARTERS):
+                    part[level, r : r + SUBLANES, q * wide + i : q * wide + i + LANES] = (
+                        product[2 * q] + product[2 * q + 1]
+                    )
 
     def groups(low, high):
+        count = max(1, -(-(high - low) // 5))
         found, at = [], low
-        while at < high:
-            size = 2 if high - at == 4 else min(3, high - at)
+        for n in range(count):
+            size = (high - at) // (count - n)
             found.append((at, size))
             at += size
         return found
 
-    def sweep(level, degree, spans):
-        source, target = levels[level][degree - 1], levels[level][degree]
+    def sweep(g, level, degree, spans):
+        source, target = term(g, level)[degree - 1], term(g, level)[degree]
         for at, size in spans:
             lanes = lax.broadcasted_iota(jnp.int32, (size, SUBLANES, LANES), 2)
             subs = lax.broadcasted_iota(jnp.int32, (size, SUBLANES, LANES), 1)
@@ -348,85 +368,93 @@
                 if degree == 1:
                     joint = 0.125 * total
                 else:
-                    joint = 0.25 * total - paired[at : at + size, :, i : i + LANES]
+                    joint = 0.25 * total - paired[g][at : at + size, :, i : i + LANES]
                 if degree < PASSES:
-                    paired[at : at + size, :, i : i + LANES] = joint
+                    paired[g][at : at + size, :, i : i + LANES] = joint
                 value = joint - field
                 for edge, absent in ((rim - 1, no_up), (rim + rows, no_down)):
                     if at <= edge < at + size:
-                        j = edge - at
                         lines = [value[row : row + 1] for row in range(size)]
-                        lines[j] = jnp.where(absent, 0.0, lines[j])
+                        lines[edge - at] = jnp.where(absent, 0.0, lines[edge - at])
                         value = jnp.concatenate(lines, axis=0)
                 target[at : at + size, :, i : i + LANES] = value
 
-    def inside(level):
-        for degree in range(1, PASSES):
-            if rim + degree < rim + rows - degree:
-                sweep(level, degree, groups(rim + degree, rim + rows - degree))
-
-    def outside(level):
+    def inside(g, level, degree):
+        low, high = rim + degree, rim + rows - degree
+        if degree < PASSES and low < high:
+            sweep(g, level, degree, groups(low, high))
+
+    def outside(g, level, degree):
+        if degree == PASSES:
+            return sweep(g, level, degree, groups(rim, rim + rows))
         middle = tall // 2
-        for degree in range(1, PASSES):
-            above = groups(degree, min(rim + degree, middle))
-            below = groups(max(rim + rows - degree, middle), tall - degree)
-            sweep(level, degree, [span for both in zip(above, below) for span in both])
-        sweep(level, PASSES, groups(rim, rim + rows))
-
-    middle = rows // 2
-    for level in range(2):
-        inside(level)
-        if level == 0:
-            swap_classes.wait_recv()
-        look_up(level)
-        if level == 1:
-            correlate_step(0, 0, rows)
-
-            @pl.when(step == 1)
-            def _():
-                swap_image(0, 0).start()
-                swap_image(0, 1).start()
-
-        up, down = rims(level)
-        pl.when(has_up)(down.wait_recv)
-        pl.when(has_down)(up.wait_recv)
-        outside(level)
-        if level == 0:
-            up, down = rims(1)
-            weigh(0, 0, rim)
-            pl.when(has_up)(up.start)
-            weigh(0, rim, rows)
-            pl.when(has_down)(down.start)
-            zero_rims(1)
-        else:
-            for piece in range(2):
-                weigh(1, piece * middle, (piece + 1) * middle)
-                correlate_step(1, piece * middle, (piece + 1) * middle)
-
-                @pl.when(step == 0)
-                def _(piece=piece):
-                    swap_image(1, piece).start()
-
+        above = groups(degree, min(rim + degree, middle))
+        below = groups(max(rim + rows - degree, middle), tall - degree)
+        sweep(g, level, degree, [span for both in zip(above, below) for span in both])
+
+    degrees = range(1, PASSES + 1)
+    for degree in degrees:
+        inside(0, 0, degree)
+        inside(1, 0, degree)
+    swap_classes.wait_recv()
+    look_up(0)
+    for g in range(2):
+        await_rims(g, 0)
+        for degree in degrees:
+            outside(g, 0, degree)
+            if g == 1:
+                inside(0, 1, degree)
+        up, down = rims(g, 1)
+        weigh(g, 0, 0, rim)
+        pl.when(has_up)(up.start)
+        weigh(g, 0, rim, rows)
+        pl.when(has_down)(down.start)
+
+    look_up(1)
+    correlate_step(0, 0, rows)
+
+    @pl.when(step == 1)
+    def _():
+        swap_image(0, 0).start()
+        swap_image(0, 1).start()
+
+    await_rims(0, 1)
+    for degree in degrees:
+        outside(0, 1, degree)
+        inside(1, 1, degree)
+    weigh(0, 1, 0, rows)
+    await_rims(1, 1)
+    for degree in degrees:
+        outside(1, 1, degree)
+    half = rows // 2
     for piece in range(2):
-        swap = swap_image(0, piece)
-        swap.wait_recv()
-        here = pl.ds(piece * middle, middle)
+        weigh(1, 1, piece * half, (piece + 1) * half)
+        correlate_step(1, piece * half, (piece + 1) * half)
+
+        @pl.when(step == 0)
+        def _(piece=piece):
+            swap_image(1, piece).start()
+
+    for piece in range(2):
+        swap_image(0, piece).wait_recv()
+        here = pl.ds(piece * half, half)
         image_ref[here] = part[step, here] + got[here]
     for piece in range(2):
         swap_image(0, piece).wait_send()
     swap_classes.wait_send()
-    for level in range(2):
-        up, down = rims(level)
-        pl.when(has_up)(up.wait_send)
-        pl.when(has_down)(down.wait_send)
+    for g in range(2):
+        for level in range(2):
+            up, down = rims(g, level)
+            pl.when(has_up)(up.wait_send)
+            pl.when(has_down)(down.wait_send)
 
 
 def in_kernel(strips, surface, velocity_class, table):
     freqs, parts, rows, full = surface.shape
-    half = full // 2
+    wide = full // QUARTERS
     tall = rows + 2 * PASSES
     f32 = jnp.float32
-    fields = pltpu.VMEM((tall, SUBLANES, half), f32)
+    fields = pltpu.VMEM((tall, SUBLANES, wide), f32)
     return pl.pallas_call(
         functools.partial(migrate, strips),
         out_shape=jax.ShapeDtypeStruct((rows, full), f32),
@@ -437,15 +465,15 @@
             pltpu.VMEM((2, rows, full), jnp.int32),
             pltpu.SMEM(table.shape, f32),
             pltpu.VMEM((2, PASSES + 1, SUBLANES, LANES), f32),
-            pltpu.VMEM((2, PASSES + 1, rows, SUBLANES, half), f32),
+            pltpu.VMEM((2, PASSES + 1, rows, SUBLANES, wide), f32),
             pltpu.VMEM((2, rows, full), f32),
             pltpu.VMEM((rows, full), f32),
         ]
-        + [fields] * (PASSES + 3)
+        + [fields] * (2 * (PASSES + 3))
         + [
             pltpu.SemaphoreType.DMA((3,)),
-            pltpu.SemaphoreType.DMA((2, 2)),
-            pltpu.SemaphoreType.DMA((2, 2)),
+            pltpu.SemaphoreType.DMA((2, 2, 2)),
+            pltpu.SemaphoreType.DMA((2, 2, 2)),
             pltpu.SemaphoreType.DMA((3,)),
             pltpu.SemaphoreType.DMA((3,)),
         ],
@@ -461,10 +489,10 @@
         mesh.shape["depth"] == 2
         and velocity_class.shape[0] == 1
         and freqs == 2
-        and 2 * parts == SUBLANES
+        and parts == 4
         and rows % (2 * SUBLANES) == 0
         and PASSES <= rows < 2 * PASSES
-        and full % (2 * LANES) == 0
+        and full % (QUARTERS * LANES) == 0
         and rows * full <= 2**15
     )
 

time: 20.8 us -> 19.4 us (0.933)
  Pallas kernels: 19.1 us -> 17.8 us
    pallas_call x1, Pallas kernels: 19.1 us -> 17.8 us  [in_kernel(): pl.pallas_call(functools.partial(migrate, strips), out_shape=jax.ShapeDty...]
where the time goes in v4:
time: 19.4 us; the launch traced here: 19.2 us
  Pallas kernels  17.8 us (92%)
  local copies, waits for them, and re-layouts  1.47 us (8%)
    pallas_call x1, Pallas kernels, in_kernel(): pl.pallas_call(functools.partial(migrate, strips), out_shape=jax.ShapeDty...  17.8 us
    unnamed x1, local copies, waits for them, and re-layouts  1.47 us

profile of v4, /device:TPU:11, one launch (start us, length us, event | category | flops | bytes accessed | tf_op | source)
XLA Modules:
  0.0 19.2 jit_solution(8747658399489738634)
XLA Ops:
  0.0 17.8 %shard_map.37 = f32[16,1024]{1,0:T(8,128)} custom-call(f32[2,4,16,1024]{3,2,1,0:T(8,128)} %surface_ref.1, s32[16,1024]{1,0:T(8,128)} %bitcast.3, f32[2,8,2,10]{3,2,1,0:T(2,128)} %table_ref.1), custom_call_target="tpu_custom_call" | custom-call | tf_op jit(solution)/shard_map/pallas_call | solution.py:458
  17.8 1.5 %copy.5 = f32[1,16,1024]{2,1,0:T(8,128)} copy(f32[1,16,1024]{2,1,0:T(8,128)} %bitcast.2) | data formatting | bytes 131072

commit v5 on v4

--- a/solution.py
+++ b/solution.py
@@ -138,24 +138,51 @@
     return lax.all_to_all(image, "depth", split_axis=0, concat_axis=2, tiled=True)
 
 
+def pick(block, index):
+    return jnp.take_along_axis(block, index, axis=1, mode="promise_in_bounds")
+
+
+def interleaved(blocks):
+    count = len(blocks)
+    lane = lax.broadcasted_iota(jnp.int32, (SUBLANES, LANES), 1)
+    found = []
+    for j in range(count):
+        index = lax.rem(lane * count + j, LANES)
+        tile = pick(blocks[0], index)
+        for n in range(1, count):
+            tile = jnp.where(lane * count >= n * LANES, pick(blocks[n], index), tile)
+        found.append(tile)
+    return found
+
+
+def restored(blocks):
+    count = len(blocks)
+    lane = lax.broadcasted_iota(jnp.int32, (SUBLANES, LANES), 1)
+    found = []
+    for n in range(count):
+        index = (lane + n * LANES) // count
+        tile = pick(blocks[0], index)
+        for j in range(1, count):
+            tile = jnp.where(lax.rem(lane, count) == j, pick(blocks[j], index), tile)
+        found.append(tile)
+    return found
+
+
 def column_sum(tiles, lane, sub):
-    rights = [pltpu.roll(t, 1, axis=2) for t in tiles]
-    lefts = [pltpu.roll(t, LANES - 1, axis=2) for t in tiles]
-    before = jnp.where(sub < 2, 0.0, pltpu.roll(rights[-1], 2, axis=1))
-    after = jnp.where(sub < SUBLANES - 2, pltpu.roll(lefts[0], SUBLANES - 2, axis=1), 0.0)
-    sums = []
-    for i, t in enumerate(tiles):
-        right = jnp.where(lane == 0, rights[i - 1] if i else before, rights[i])
-        left = jnp.where(lane == LANES - 1, lefts[i + 1] if i + 1 < len(tiles) else after, lefts[i])
-        sums.append((right + left) + (t + t))
-    return sums
+    right = pltpu.roll(tiles[-1], 1, axis=2)
+    left = pltpu.roll(tiles[0], LANES - 1, axis=2)
+    before = jnp.where(sub < 2, 0.0, pltpu.roll(right, 2, axis=1))
+    after = jnp.where(sub < SUBLANES - 2, pltpu.roll(left, SUBLANES - 2, axis=1), 0.0)
+    line = [jnp.where(lane == 0, before, right)] + tiles + [jnp.where(lane == LANES - 1, after, left)]
+    pairs = [p + q for p, q in zip(line[:-1], line[1:])]
+    return [p + q for p, q in zip(pairs[:-1], pairs[1:])]
 
 
 def migrate(strips, surface_ref, velocity_ref, table_ref, image_ref, *scratch):
-    raw, classes, numbers, coef, spot, part, got = scratch[:7]
+    raw, classes, numbers, coef, spot, part, got, mixed = scratch[:8]
     per_group = PASSES + 3
-    held = [scratch[7 + g * per_group : 7 + (g + 1) * per_group] for g in range(2)]
-    load_sem, rim_send, rim_recv, swap_send, swap_recv = scratch[7 + 2 * per_group :]
+    held = [scratch[8 + g * per_group : 8 + (g + 1) * per_group] for g in range(2)]
+    load_sem, rim_send, rim_recv, swap_send, swap_recv = scratch[8 + 2 * per_group :]
     first = [h[0] for h in held]
     second = [h[1] for h in held]
     paired = [h[2] for h in held]
@@ -200,14 +227,18 @@
     load_surface.wait()
     for g in range(2):
         for r in range(0, rows, SUBLANES):
-            for i in tiles:
-                block = jnp.concatenate(
+            parts = [
+                interleaved(
                     [
-                        raw[2 * g : 2 * g + 2, r : r + SUBLANES, q * wide + i : q * wide + i + LANES]
-                        for q in range(QUARTERS)
-                    ],
-                    axis=0,
+                        raw[2 * g + c, r : r + SUBLANES, q * wide + i : q * wide + i + LANES]
+                        for i in tiles
+                    ]
                 )
+                for q in range(QUARTERS)
+                for c in range(2)
+            ]
+            for j, i in enumerate(tiles):
+                block = jnp.stack([part_tiles[j] for part_tiles in parts])
                 first[g][rim + r : rim + r + SUBLANES, :, i : i + LANES] = jnp.swapaxes(block, 0, 1)
 
     load_classes.wait()
@@ -290,10 +321,21 @@
     lax.fori_loop(0, PASSES + 1, fill, 0)
 
     def look_up(level):
+        for r in range(0, rows, SUBLANES):
+            for q in range(QUARTERS):
+                found = interleaved(
+                    [
+                        classes[level, r : r + SUBLANES, q * wide + i : q * wide + i + LANES]
+                        for i in tiles
+                    ]
+                )
+                for i, tile in zip(tiles, found):
+                    mixed[r : r + SUBLANES, q * wide + i : q * wide + i + LANES] = tile
+
         def block(b, carry):
             for j in range(4):
                 r = b * 4 + j
-                kind = classes[level, pl.ds(r, 1), :]
+                kind = mixed[pl.ds(r, 1), :]
                 for i in tiles:
                     index = None
                     for q in range(QUARTERS):
@@ -437,8 +479,13 @@
 
     for piece in range(2):
         swap_image(0, piece).wait_recv()
-        here = pl.ds(piece * half, half)
-        image_ref[here] = part[step, here] + got[here]
+        for r in range(piece * half, (piece + 1) * half, SUBLANES):
+            here = slice(r, r + SUBLANES)
+            for q in range(QUARTERS):
+                places = [slice(q * wide + i, q * wide + i + LANES) for i in tiles]
+                found = restored([part[step, here, place] + got[here, place] for place in places])
+                for place, tile in zip(places, found):
+                    image_ref[here, place] = tile
     for piece in range(2):
         swap_image(0, piece).wait_send()
     swap_classes.wait_send()
@@ -468,6 +515,7 @@
             pltpu.VMEM((2, PASSES + 1, rows, SUBLANES, wide), f32),
             pltpu.VMEM((2, rows, full), f32),
             pltpu.VMEM((rows, full), f32),
+            pltpu.VMEM((rows, full), jnp.int32),
         ]
         + [fields] * (2 * (PASSES + 3))
         + [
@@ -493,6 +541,7 @@
         and rows % (2 * SUBLANES) == 0
         and PASSES <= rows < 2 * PASSES
         and full % (QUARTERS * LANES) == 0
+        and LANES % (full // (QUARTERS * LANES)) == 0
         and rows * full <= 2**15
     )
 

time: 19.4 us -> 18.9 us (0.974)
  Pallas kernels: 17.8 us -> 17.2 us
    pallas_call x1, Pallas kernels: 17.8 us -> 17.2 us  [in_kernel(): pl.pallas_call(functools.partial(migrate, strips), out_shape=jax.ShapeDty...]
where the time goes in v5:
time: 18.9 us; the launch traced here: 18.7 us
  Pallas kernels  17.2 us (91%)
  local copies, waits for them, and re-layouts  1.47 us (8%)
    pallas_call x1, Pallas kernels, in_kernel(): pl.pallas_call(functools.partial(migrate, strips), out_shape=jax.ShapeDty...  17.2 us
    unnamed x1, local copies, waits for them, and re-layouts  1.47 us

profile of v5, /device:TPU:11, one launch (start us, length us, event | category | flops | bytes accessed | tf_op | source)
XLA Modules:
  0.0 18.7 jit_solution(6564961771536478249)
XLA Ops:
  0.0 17.2 %shard_map.37 = f32[16,1024]{1,0:T(8,128)} custom-call(f32[2,4,16,1024]{3,2,1,0:T(8,128)} %surface_ref.1, s32[16,1024]{1,0:T(8,128)} %bitcast.3, f32[2,8,2,10]{3,2,1,0:T(2,128)} %table_ref.1), custom_call_target="tpu_custom_call" | custom-call | tf_op jit(solution)/shard_map/pallas_call | solution.py:505
  17.2 1.5 %copy.5 = f32[1,16,1024]{2,1,0:T(8,128)} copy(f32[1,16,1024]{2,1,0:T(8,128)} %bitcast.2) | data formatting | bytes 131072

commit v6 on v5

--- a/solution.py
+++ b/solution.py
@@ -178,11 +178,11 @@
     return [p + q for p, q in zip(pairs[:-1], pairs[1:])]
 
 
-def migrate(strips, surface_ref, velocity_ref, table_ref, image_ref, *scratch):
-    raw, classes, numbers, coef, spot, part, got, mixed = scratch[:8]
+def migrate(strips, surface_ref, velocity_ref, table_ref, own_ref, got_ref, *scratch):
+    raw, classes, numbers, coef, spot, part, mixed = scratch[:7]
     per_group = PASSES + 3
-    held = [scratch[8 + g * per_group : 8 + (g + 1) * per_group] for g in range(2)]
-    load_sem, rim_send, rim_recv, swap_send, swap_recv = scratch[8 + 2 * per_group :]
+    held = [scratch[7 + g * per_group : 7 + (g + 1) * per_group] for g in range(2)]
+    load_sem, rim_send, rim_recv, swap_send, swap_recv = scratch[7 + 2 * per_group :]
     first = [h[0] for h in held]
     second = [h[1] for h in held]
     paired = [h[2] for h in held]
@@ -284,7 +284,7 @@
         here = pl.ds(piece * (rows // 2), rows // 2)
         return pltpu.make_async_remote_copy(
             src_ref=part.at[level, here],
-            dst_ref=got.at[here],
+            dst_ref=got_ref.at[here],
             send_sem=swap_send.at[1 + piece],
             recv_sem=swap_recv.at[1 + piece],
             device_id={"depth": other},
@@ -375,15 +375,16 @@
 
     def correlate_step(level, low, high):
         for r in range(low, high, SUBLANES):
+            products = []
             for i in tiles:
                 source, receiver = (
                     results[level][g][rim + r : rim + r + SUBLANES, :, i : i + LANES] for g in range(2)
                 )
-                product = jnp.swapaxes(source * receiver, 0, 1)
-                for q in range(QUARTERS):
-                    part[level, r : r + SUBLANES, q * wide + i : q * wide + i + LANES] = (
-                        product[2 * q] + product[2 * q + 1]
-                    )
+                products.append(jnp.swapaxes(source * receiver, 0, 1))
+            for q in range(QUARTERS):
+                found = restored([p[2 * q] + p[2 * q + 1] for p in products])
+                for i, tile in zip(tiles, found):
+                    part[level, r : r + SUBLANES, q * wide + i : q * wide + i + LANES] = tile
 
     def groups(low, high):
         count = max(1, -(-(high - low) // 5))
@@ -460,6 +461,10 @@
         swap_image(0, 0).start()
         swap_image(0, 1).start()
 
+    @pl.when(step == 0)
+    def _():
+        pltpu.make_async_copy(part.at[0], own_ref, load_sem.at[3]).start()
+
     await_rims(0, 1)
     for degree in degrees:
         outside(0, 1, degree)
@@ -477,17 +482,14 @@
         def _(piece=piece):
             swap_image(1, piece).start()
 
-    for piece in range(2):
-        swap_image(0, piece).wait_recv()
-        for r in range(piece * half, (piece + 1) * half, SUBLANES):
-            here = slice(r, r + SUBLANES)
-            for q in range(QUARTERS):
-                places = [slice(q * wide + i, q * wide + i + LANES) for i in tiles]
-                found = restored([part[step, here, place] + got[here, place] for place in places])
-                for place, tile in zip(places, found):
-                    image_ref[here, place] = tile
+    @pl.when(step == 1)
+    def _():
+        pltpu.make_async_copy(part.at[1], own_ref, load_sem.at[3]).start()
+
     for piece in range(2):
         swap_image(0, piece).wait_send()
+        swap_image(0, piece).wait_recv()
+    pltpu.make_async_copy(part.at[0], own_ref, load_sem.at[3]).wait()
     swap_classes.wait_send()
     for g in range(2):
         for level in range(2):
@@ -502,11 +504,11 @@
     tall = rows + 2 * PASSES
     f32 = jnp.float32
     fields = pltpu.VMEM((tall, SUBLANES, wide), f32)
-    return pl.pallas_call(
+    own, got = pl.pallas_call(
         functools.partial(migrate, strips),
-        out_shape=jax.ShapeDtypeStruct((rows, full), f32),
+        out_shape=[jax.ShapeDtypeStruct((rows, full), f32)] * 2,
         in_specs=[pl.BlockSpec(memory_space=pl.ANY)] * 3,
-        out_specs=pl.BlockSpec(memory_space=pltpu.VMEM),
+        out_specs=[pl.BlockSpec(memory_space=pl.ANY)] * 2,
         scratch_shapes=[
             pltpu.VMEM((parts, rows, full), f32),
             pltpu.VMEM((2, rows, full), jnp.int32),
@@ -514,12 +516,11 @@
             pltpu.VMEM((2, PASSES + 1, SUBLANES, LANES), f32),
             pltpu.VMEM((2, PASSES + 1, rows, SUBLANES, wide), f32),
             pltpu.VMEM((2, rows, full), f32),
-            pltpu.VMEM((rows, full), f32),
             pltpu.VMEM((rows, full), jnp.int32),
         ]
         + [fields] * (2 * (PASSES + 3))
         + [
-            pltpu.SemaphoreType.DMA((3,)),
+            pltpu.SemaphoreType.DMA((4,)),
             pltpu.SemaphoreType.DMA((2, 2, 2)),
             pltpu.SemaphoreType.DMA((2, 2, 2)),
             pltpu.SemaphoreType.DMA((3,)),
@@ -528,7 +529,8 @@
         compiler_params=pltpu.CompilerParams(
             collective_id=0, has_side_effects=True, vmem_limit_bytes=56 * 2**20
         ),
-    )(surface, velocity_class.reshape(rows, full), table)[None]
+    )(surface, velocity_class.reshape(rows, full), table)
+    return (own + got)[None]
 
 
 def fits(mesh, surface, velocity_class):

time: 18.9 us -> 18.5 us (0.979)
  other arithmetic: 0 us -> 1.51 us
  local copies, waits for them, and re-layouts: 1.47 us -> 0 us
  Pallas kernels: 17.2 us -> 16.9 us
    broadcast_in_dim x0 -> x1, other arithmetic: none -> 1.51 us  [in_kernel(): return (own + got)[None]]
    unnamed x1 -> x0, local copies, waits for them, and re-layouts: 1.47 us -> none
    pallas_call x1, Pallas kernels: 17.2 us -> 16.9 us  [in_kernel(): pl.pallas_call(functools.partial(migrate, strips), out_shape=[jax.ShapeDt...]
where the time goes in v6:
time: 18.5 us; the launch traced here: 18.4 us
  Pallas kernels  16.9 us (91%)
  other arithmetic  1.51 us (8%)
    pallas_call x1, Pallas kernels, in_kernel(): pl.pallas_call(functools.partial(migrate, strips), out_shape=[jax.ShapeDt...  16.9 us
    broadcast_in_dim x1, other arithmetic, in_kernel(): return (own + got)[None]  1.51 us

profile of v6, /device:TPU:11, one launch (start us, length us, event | category | flops | bytes accessed | tf_op | source)
XLA Modules:
  0.0 18.4 jit_solution(17501387389106688528)
XLA Ops:
  0.0 16.9 %shard_map.37 = (f32[16,1024]{1,0:T(8,128)}, f32[16,1024]{1,0:T(8,128)}) custom-call(f32[2,4,16,1024]{3,2,1,0:T(8,128)} %surface_ref.1, s32[16,1024]{1,0:T(8,128)} %bitcast.3, f32[2,8,2,10]{3,2,1,0:T(2,128)} %table_ref.1), custom_call_target="tpu_custom_call" | custom-call | tf_op jit(solution)/shard_map/pallas_call | solution.py:507
  16.9 1.5 %add_bitcast_fusion = f32[1,16,1024]{2,1,0:T(8,128)} fusion(f32[16,1024]{1,0:T(8,128)} %get-tuple-element.7, f32[16,1024]{1,0:T(8,128)} %get-tuple-element.8), kind=kLoop, calls=%fused_computation | loop fusion | flops 16384 | bytes 196608 | tf_op jit(solution)/shard_map/broadcast_in_dim | solution.py:533

commit v7 on v6

--- a/solution.py
+++ b/solution.py
@@ -291,10 +291,9 @@
             device_id_type=MESH,
         )
 
-    for g in range(2):
-        up, down = rims(g, 0)
-        pl.when(has_up)(up.start)
-        pl.when(has_down)(down.start)
+    up, down = rims(0, 0)
+    pl.when(has_up)(up.start)
+    pl.when(has_down)(down.start)
     swap_classes = pltpu.make_async_remote_copy(
         src_ref=classes.at[step],
         dst_ref=classes.at[step],
@@ -436,6 +435,12 @@
         sweep(g, level, degree, [span for both in zip(above, below) for span in both])
 
     degrees = range(1, PASSES + 1)
+    up, down = rims(0, 0)
+    pl.when(has_up)(up.wait_send)
+    pl.when(has_down)(down.wait_send)
+    up, down = rims(1, 0)
+    pl.when(has_up)(up.start)
+    pl.when(has_down)(down.start)
     for degree in degrees:
         inside(0, 0, degree)
         inside(1, 0, degree)
@@ -491,11 +496,10 @@
         swap_image(0, piece).wait_recv()
     pltpu.make_async_copy(part.at[0], own_ref, load_sem.at[3]).wait()
     swap_classes.wait_send()
-    for g in range(2):
-        for level in range(2):
-            up, down = rims(g, level)
-            pl.when(has_up)(up.wait_send)
-            pl.when(has_down)(down.wait_send)
+    for g, level in ((1, 0), (0, 1), (1, 1)):
+        up, down = rims(g, level)
+        pl.when(has_up)(up.wait_send)
+        pl.when(has_down)(down.wait_send)
 
 
 def in_kernel(strips, surface, velocity_class, table):

time: 18.5 us -> 18.5 us (level)
  no operation moved by 1% of the time
where the time goes in v7:
time: 18.5 us; the launch traced here: 18.4 us
  Pallas kernels  16.8 us (91%)
  other arithmetic  1.51 us (8%)
    pallas_call x1, Pallas kernels, in_kernel(): pl.pallas_call(functools.partial(migrate, strips), out_shape=[jax.ShapeDt...  16.8 us
    broadcast_in_dim x1, other arithmetic, in_kernel(): return (own + got)[None]  1.51 us

profile of v7, /device:TPU:11, one launch (start us, length us, event | category | flops | bytes accessed | tf_op | source)
XLA Modules:
  0.0 18.4 jit_solution(6164875888069102256)
XLA Ops:
  0.0 16.8 %shard_map.37 = (f32[16,1024]{1,0:T(8,128)}, f32[16,1024]{1,0:T(8,128)}) custom-call(f32[2,4,16,1024]{3,2,1,0:T(8,128)} %surface_ref.1, s32[16,1024]{1,0:T(8,128)} %bitcast.3, f32[2,8,2,10]{3,2,1,0:T(2,128)} %table_ref.1), custom_call_target="tpu_custom_call" | custom-call | tf_op jit(solution)/shard_map/pallas_call | solution.py:511
  16.9 1.5 %add_bitcast_fusion = f32[1,16,1024]{2,1,0:T(8,128)} fusion(f32[16,1024]{1,0:T(8,128)} %get-tuple-element.7, f32[16,1024]{1,0:T(8,128)} %get-tuple-element.8), kind=kLoop, calls=%fused_computation | loop fusion | flops 16384 | bytes 196608 | tf_op jit(solution)/shard_map/broadcast_in_dim | solution.py:537
